TPU v7x, 256 devices: a whole 4x4x8 slice. The times are simulated.
256 devices in a mesh: blk: 16 (over z, y_lo), rep: 16 (over y_hi, x, core).
Axes of the slice: x: 4, y: 4 (y_hi: 2, y_lo: 2; y = y_hi * 2 + y_lo), z: 8, core: 2. Of those that a mesh axis runs over, the one named last changes fastest.
Arguments:
- features: bfloat16 [65536, 256], P(('blk', 'rep')), may hold values from -6 to 6
- w_self: bfloat16 [256, 256], replicated, may hold values from -0.375 to 0.375
- w_neigh: bfloat16 [256, 256], replicated, may hold values from -0.375 to 0.375
- bias: float32 [256], replicated, may hold values from -3 to 3
- cotangent: bfloat16 [65536, 256], P(('blk', 'rep')), may hold values from -6 to 6
- tile_values: bfloat16 [16, 16, 16, 12, 128, 128], P('blk', 'rep')
- tile_rows: int32 [16, 16, 16, 12], P('blk', 'rep'), may hold values from 0 to 31, as said below
- tile_cols: int32 [16, 16, 16, 12], P('blk', 'rep'), may hold values from 0 to 1
- tile_counts: int32 [16, 16, 16], P('blk', 'rep'), may hold values from 1 to 12, as said below
Outputs:
- output: bfloat16 [65536, 256], P(('blk', 'rep'))
- grad_features: bfloat16 [65536, 256], P(('blk', 'rep'))
- grad_self: float32 [256, 256], replicated
- grad_neigh: float32 [256, 256], replicated
- grad_bias: float32 [256], replicated
Inputs may be any that keep to these rules, and one draw needn't show every extreme that they name: Among the live slots s < tile_counts[b, r, c] of one b, r, c, the pairs (tile_rows, tile_cols) are distinct; slots from tile_counts[b, r, c] on are not part of the adjacency. `tile_counts`: some entry equals 12 in every draw.
All inputs are finite; a program needn't handle non-finite values.
Results may differ from a plain program's by a relative error of at most 0.02.
Values may be sent and summed in bfloat16 or wider, within the bound.
No kernel may reach another device: no remote copies, remote signals or barrier semaphores. Data moves between devices by JAX's collectives and lax.ppermute only.
A program may use at most 64 MiB of HBM per device.

v0:
```python
import jax
import jax.numpy as jnp
from jax import lax
from jax.sharding import PartitionSpec as P


def dense_layer(x_rows, agg_rows, cot_rows, w_self, w_neigh, bias):
    zvals = (
        jnp.dot(x_rows, w_self, preferred_element_type=jnp.float32)
        + jnp.dot(agg_rows, w_neigh, preferred_element_type=jnp.float32)
        + bias
    )
    sig = jax.nn.sigmoid(zvals)
    output = (zvals * sig).astype(jnp.bfloat16)
    grad_z = (cot_rows.astype(jnp.float32) * sig * (1.0 + zvals * (1.0 - sig))).astype(jnp.bfloat16)
    grad_agg = jnp.einsum("ng,fg->nf", grad_z, w_neigh, preferred_element_type=jnp.float32).astype(
        jnp.bfloat16
    )
    return (output, grad_z, grad_agg)


def local(
    features, w_self, w_neigh, bias, cotangent, tile_values, tile_rows, tile_cols, tile_counts
):
    rows_dev = features.shape[0]
    width = features.shape[1]
    values = tile_values[0, 0]
    row_ids = tile_rows[0, 0]
    col_ids = tile_cols[0, 0]
    counts = tile_counts[0, 0]
    slots = values.shape[1]
    tile = values.shape[2]
    per_dev = rows_dev // tile
    nblk = lax.axis_size("blk")
    nrep = lax.axis_size("rep")
    alive_all = lax.broadcasted_iota(jnp.int32, (nblk, slots), 1) < counts[:, None]

    def slot_data(block):
        vals = lax.dynamic_index_in_dim(values, block, 0, keepdims=False)
        rows_here = lax.dynamic_index_in_dim(row_ids, block, 0, keepdims=False)
        cols_here = lax.dynamic_index_in_dim(col_ids, block, 0, keepdims=False)
        alive = lax.dynamic_index_in_dim(alive_all, block, 0, keepdims=False)
        return (vals, rows_here, cols_here, alive)

    empty = jnp.zeros((nrep * per_dev, tile, width), jnp.float32)
    piece = lax.all_gather(features, "blk", axis=0, tiled=True)
    tiles = piece.reshape(piece.shape[0] // tile, tile, width)

    def add_one_block(j, acc):
        vals, rows_here, cols_here, alive = slot_data(j)
        picked = jnp.take(tiles, j * per_dev + cols_here, axis=0)
        prod = jnp.einsum("sij,sjf->sif", vals, picked, preferred_element_type=jnp.float32)
        prod = jnp.where(alive[:, None, None], prod, 0.0)
        return acc.at[rows_here].add(prod)

    partial_value = lax.fori_loop(0, piece.shape[0] // rows_dev, add_one_block, empty)
    partial_value = partial_value.reshape(nrep * rows_dev, width)
    agg_sum = lax.psum_scatter(
        partial_value.astype(jnp.bfloat16), "rep", scatter_dimension=0, tiled=True
    )
    output, grad_z, grad_agg = dense_layer(features, agg_sum, cotangent, w_self, w_neigh, bias)
    grad_agg_full = lax.all_gather(grad_agg, "rep", axis=0, tiled=True)
    grad_tiles = grad_agg_full.reshape(nrep * per_dev, tile, width)
    grad_self, grad_neigh, grad_bias = lax.psum(
        (
            jnp.einsum("nf,ng->fg", features, grad_z, preferred_element_type=jnp.float32),
            jnp.einsum("nf,ng->fg", agg_sum, grad_z, preferred_element_type=jnp.float32),
            jnp.sum(grad_z.astype(jnp.float32), axis=0),
        ),
        ("blk", "rep"),
    )
    nblocks = rows_dev * lax.axis_size("blk") // rows_dev

    def column_one_block(j, acc):
        vals, rows_here, cols_here, alive = slot_data(j)
        picked = jnp.take(grad_tiles, rows_here, axis=0)
        term = jnp.einsum("sji,sjf->sif", vals, picked, preferred_element_type=jnp.float32)
        term = jnp.where(alive[:, None, None], term, 0.0)
        return acc.at[j * per_dev + cols_here].add(term)

    start_acc = jnp.zeros((nblocks * per_dev, tile, width), jnp.float32)
    spread = lax.psum_scatter(
        lax.fori_loop(0, nblocks, column_one_block, start_acc)
        .reshape(rows_dev * lax.axis_size("blk"), width)
        .astype(jnp.bfloat16),
        "blk",
        scatter_dimension=0,
        tiled=True,
    ).astype(jnp.float32)
    own = jnp.einsum("ng,fg->nf", grad_z, w_self, preferred_element_type=jnp.float32)
    grad_features = (own + spread).astype(jnp.bfloat16)
    return (output, grad_features, grad_self, grad_neigh, grad_bias)


def solution(mesh):
    in_specs = (
        P(("blk", "rep"), None),
        P(),
        P(),
        P(),
        P(("blk", "rep"), None),
        P("blk", "rep", None, None, None, None),
        P("blk", "rep", None, None),
        P("blk", "rep", None, None),
        P("blk", "rep", None),
    )
    out_specs = (P(("blk", "rep"), None), P(("blk", "rep"), None), P(), P(), P())
    return jax.shard_map(local, mesh=mesh, in_specs=in_specs, out_specs=out_specs, check_vma=False)
```

profile of v0, /device:TPU:8, one launch (start us, length us, event | category | flops | bytes accessed | tf_op | source)
XLA Modules:
  0.0 690.5 jit_solution(6258346547114127622)
XLA Ops:
  10.2 74.2 %all-gather.3.cloned.1.call-done = bf16[4096,256]{1,0:T(8,128)(2,1)} async-done(((bf16[256,256]{1,0:T(8,128)(2,1)}), bf16[4096,256]{1,0:T(8,128)(2,1)}) %all-gather.3.cloned.1.call-update) | async-done | bytes 2097168 | tf_op jit(solution)/shard_map/all_gather | solution.py:46
  86.8 124.6 %while.26 = (s32[]{:T(128)}, f32[32,128,256]{2,1,0:T(8,128)}, s32[16,12]{1,0:T(8,128)S(1)}, pred[16,12]{1,0:T(8,128)(4,1)S(1)}, bf16[16,12,128,128]{3,2,1,0:T(8,...) while((s32[]{:T(128)}, f32[32,128,256]{2,1,0:T(8,128)}, ...), condition=%wide.region_2.4_spmd, body=%wide.region_0.3_spmd.sunk | while | flops 101844088 | bytes 9048593 | solution.py:56
  137.2 4.1 scatter_fusion
  152.8 4.1 scatter_fusion
  191.7 4.2 scatter_fusion
  199.5 4.1 scatter_fusion
  215.6 76.9 %reduce-scatter.3.cloned.1.call-done = bf16[256,256]{1,0:T(8,128)(2,1)} async-done(((bf16[4096,256]{1,0:T(8,128)(2,1)}), bf16[256,256]{1,0:T(8,128)(2,1)}) %reduce-scatter.3.cloned.1.call-update) | async-done | bytes 131088 | tf_op jit(solution)/shard_map/reduce_scatter | solution.py:58
  295.3 8.6 %copy.15 = bf16[1,1,16,12,128,128]{4,5,3,2,1,0:T(8,128)(2,1)} copy(bf16[1,1,16,12,128,128]{5,4,3,2,1,0:T(8,128)(2,1)} %bitcast.76) | data formatting | bytes 12582912 | tf_op args[5]
  305.9 42.4 %all-gather.5.cloned.1.call-done = bf16[4096,256]{1,0:T(8,128)(2,1)} async-done(((bf16[256,256]{1,0:T(8,128)(2,1)}), bf16[4096,256]{1,0:T(8,128)(2,1)}) %all-gather.5.cloned.1.call-update) | async-done | bytes 2097168 | tf_op jit(solution)/shard_map/all_gather | solution.py:62
  350.8 125.4 %while.27 = (s32[]{:T(128)}, f32[32,128,256]{2,1,0:T(8,128)}, s32[16,12]{1,0:T(8,128)S(1)}, pred[16,12]{1,0:T(8,128)(4,1)S(1)}, bf16[16,12,128,128]{2,3,1,0:T(8,...) while((s32[]{:T(128)}, f32[32,128,256]{2,1,0:T(8,128)}, ...), condition=%wide.region_6.8_spmd, body=%wide.region_4.7_spmd.sunk | while | flops 101844088 | bytes 9048593 | solution.py:83
  354.5 4.2 scatter_fusion.1
  362.3 4.1 scatter_fusion.1
  370.1 4.1 scatter_fusion.1
  378.0 4.1 scatter_fusion.1
  385.8 4.2 scatter_fusion.1
  393.7 4.2 scatter_fusion.1
  401.7 4.2 scatter_fusion.1
  409.5 4.3 scatter_fusion.1
  433.0 4.1 scatter_fusion.1
  440.9 4.3 scatter_fusion.1
  456.5 4.2 scatter_fusion.1
  480.0 77.0 %psum.23 = f32[256]{0:T(256)} all-reduce(f32[256]{0:T(256)S(1)} %get-tuple-element.302), channel_id=1, replica_groups=mesh['blk'=16,'rep'=16] {'blk','rep'}, use_global_device_ids=true, to_apply=%region_11.13 | all-reduce | flops 256 | bytes 2048 | tf_op jit(solution)/shard_map/psum | solution.py:64
  557.0 49.7 %all-reduce.3.cloned.1.call-done = (f32[256,256]{0,1:T(8,128)}, f32[256,256]{1,0:T(8,128)}) async-done(((f32[256,256]{0,1:T(8,128)}, f32[256,256]{1,0:T(8,128)}), (f32[256,256]{0,1:T(8,128)}, f32[256,256]{1,0:T(8,128)})) %all-reduce.3.cloned.1.call-update) | async-done | bytes 524304 | tf_op jit(solution)/shard_map/psum | solution.py:64
  608.5 72.0 %reduce-scatter.5.cloned.1.call-done = bf16[256,256]{1,0:T(8,128)(2,1)} async-done(((bf16[4096,256]{1,0:T(8,128)(2,1)}), bf16[256,256]{1,0:T(8,128)(2,1)}) %reduce-scatter.5.cloned.1.call-update) | async-done | bytes 131088 | tf_op jit(solution)/shard_map/reduce_scatter | solution.py:82
  (246 shorter events, 212.2 us)
Async XLA Ops:
  7.2 285.3 %copy-start = (bf16[256,256]{1,0:T(8,128)(2,1)S(1)}, bf16[256,256]{1,0:T(8,128)(2,1)}, u32[]{:S(2)}) copy-start(bf16[256,256]{1,0:T(8,128)(2,1)} %param.17) | copy-start | bytes 393220
  7.2 77.2 %all-gather.3.cloned.1.call-start = ((), (), s32[]{:S(2)}) async-start(), calls=%async_computation.2 | async-start | bytes 2228224 | tf_op jit(solution)/shard_map/all_gather | solution.py:46
  7.9 284.6 %reduce-scatter.3.cloned.1.call-start = ((), (), s32[]{:S(2)}) async-start(), calls=%async_computation.3 | async-start | bytes 2228224 | tf_op jit(solution)/shard_map/reduce_scatter | solution.py:58
  211.4 4.0 copy-start.1
  211.4 4.0 copy-start.2
  211.4 81.1 %copy-start.4 = (bf16[256,256]{1,0:T(8,128)(2,1)S(1)}, bf16[256,256]{1,0:T(8,128)(2,1)}, u32[]{:S(2)}) copy-start(bf16[256,256]{1,0:T(8,128)(2,1)} %param.19) | copy-start | bytes 393220
  211.4 81.1 %copy-start.5 = (f32[256]{0:T(256)S(1)}, f32[256]{0:T(256)}, u32[]{:S(2)}) copy-start(f32[256]{0:T(256)} %param.18) | copy-start | bytes 3076
  215.3 132.9 %all-gather.5.cloned.1.call-start = ((), (), s32[]{:S(2)}) async-start(), calls=%async_computation.4 | async-start | bytes 2228224 | tf_op jit(solution)/shard_map/all_gather | solution.py:62
  295.3 9.6 %copy-start.3 = (bf16[256,256]{1,0:T(8,128)(2,1)S(1)}, bf16[256,256]{1,0:T(8,128)(2,1)}, u32[]{:S(2)}) copy-start(bf16[256,256]{1,0:T(8,128)(2,1)} %reduce-scatter.3.cloned.1.call-done) | copy-start | bytes 393220
  295.3 311.5 %all-reduce.3.cloned.1.call-start = ((), (), s32[]{:S(2)}) async-start(), calls=%async_computation.6 | async-start | bytes 1048576 | tf_op jit(solution)/shard_map/psum | solution.py:64
  305.8 374.7 %reduce-scatter.5.cloned.1.call-start = ((), (), s32[]{:S(2)}) async-start(), calls=%async_computation.5 | async-start | bytes 2228224 | tf_op jit(solution)/shard_map/reduce_scatter | solution.py:82
Sparse Core Ops, SparseCore 0:
  9.8 74.5 all-gather.2
  215.5 77.0 reduce-scatter.2
  295.8 52.4 all-gather.4
  354.3 252.3 all-reduce.2
  609.1 71.3 reduce-scatter.4
where the time goes:
time: 697 us; the launch traced here: 691 us
  waiting for transfers between devices  316 us (45%)
  other arithmetic  141 us (20%)
  local copies, waits for them, and re-layouts  89.1 us (13%)
  blocking collectives  77 us (11%)
  matrix products  52.5 us (8%)
  between operations  13.8 us (2%)
    psum x1, blocking collectives, local(): lax.psum((jnp.einsum('nf,ng->fg', features, grad_z, preferred_element_typ...  77 us
    reduce_scatter x1, waiting for transfers between devices, local(): lax.psum_scatter(partial_value.astype(jnp.bfloat16), 'rep', scatter_dimen...  76.9 us
    all_gather x1, waiting for transfers between devices, local(): piece = lax.all_gather(features, 'blk', axis=0, tiled=True)  74.2 us
    reduce_scatter x1, waiting for transfers between devices, local(): lax.psum_scatter(lax.fori_loop(0, nblocks, column_one_block, start_acc).r...  72 us
    scatter-add x16, other arithmetic, column_one_block(): return acc.at[j * per_dev + cols_here].add(term)  66.1 us
    scatter-add x16, other arithmetic, add_one_block(): return acc.at[rows_here].add(prod)  65.5 us
    psum x1, waiting for transfers between devices, local(): lax.psum((jnp.einsum('nf,ng->fg', features, grad_z, preferred_element_typ...  49.7 us
    all_gather x1, waiting for transfers between devices, local(): grad_agg_full = lax.all_gather(grad_agg, 'rep', axis=0, tiled=True)  42.4 us
  transfers between devices with their start and end apart: 5, of which 5 were waited for; matrix products, arithmetic and copies ran while one was open for 21% of the time, Pallas kernels for 0%

commit v1 on v0

v1 whole, which is shorter than its diff:
```python
import jax
import jax.numpy as jnp
from jax import lax
from jax.experimental import pallas as pl
from jax.experimental.pallas import tpu as pltpu
from jax.sharding import PartitionSpec as P

F32 = jnp.float32
BF16 = jnp.bfloat16
NZ, NYL, NYH, NX, NC = 8, 2, 2, 4, 2
TILE = 128
SMEM = pl.BlockSpec(memory_space=pltpu.SMEM)
VMEM = pl.BlockSpec(memory_space=pltpu.VMEM)
MB = 1024 * 1024


def permute(value, dz=0, dyl=0, dyh=0, dx=0, dc=0):
    pairs = []
    for z in range(NZ):
        to_z = (z + (dz(z) if callable(dz) else dz)) % NZ
        for yl in range(NYL):
            for yh in range(NYH):
                for x in range(NX):
                    to_x = (x + (dx(x) if callable(dx) else dx)) % NX
                    for c in range(NC):
                        src = (((z * NYL + yl) * NYH + yh) * NX + x) * NC + c
                        dst = (((to_z * NYL + (yl + dyl) % NYL) * NYH + (yh + dyh) % NYH) * NX + to_x) * NC
                        pairs.append((src, dst + (c + dc) % NC))
    return lax.ppermute(value, ("blk", "rep"), pairs)


def params(mib):
    return pltpu.CompilerParams(vmem_limit_bytes=mib * MB)


def axes():
    b, r = lax.axis_index("blk"), lax.axis_index("rep")
    return b >> 1, b & 1, r >> 3, (r >> 1) & 3, r & 1


SETS = (
    ((0, 0), (0, 1), (1, 0), (1, 1), (-1, 0), (-1, 1)),
    ((2, 0), (2, 1), (-2, 0), (-2, 1)),
    ((3, 0), (3, 1), (-3, 0), (-3, 1)),
    ((4, 0), (4, 1)),
)
UNROLL = 16
LIST = 6 * 12 + UNROLL
ROW_TILES = 32


def list_body(rows_ref, cols_ref, cnt_ref, list_ref, len_ref):
    z, yl, yh, x, core = axes()
    slots = rows_ref.shape[1]
    for k, offsets in enumerate(SETS):
        n = jnp.int32(0)
        for i, (dz, dy) in enumerate(offsets):
            c = ((z + dz + NZ) & (NZ - 1)) * 2 + (yl ^ dy)

            def put(s, _, c=c, i=i, k=k, n=n):
                row = rows_ref[c, s]
                q = row >> 1
                place = (((q & 1) ^ core) * 4 + (((q >> 1) - x) & 3)) * 2 + ((q >> 3) ^ yh)
                place = place * 2 + (row & 1)
                near = i * 2 + cols_ref[c, s]
                list_ref[k, n + s] = (c * slots + s) | (near << 8) | (place << 16)
                return 0

            lax.fori_loop(0, cnt_ref[c], put, 0)
            n = n + cnt_ref[c]
        len_ref[k] = (n + UNROLL - 1) // UNROLL
        for s in range(UNROLL):
            list_ref[k, n + s] = ((2 * len(offsets)) << 8) | (ROW_TILES << 16)


def list_kernel(rows, cols, counts):
    return pl.pallas_call(
        list_body,
        out_shape=[
            jax.ShapeDtypeStruct((len(SETS), LIST), jnp.int32),
            jax.ShapeDtypeStruct((len(SETS),), jnp.int32),
        ],
        in_specs=[SMEM] * 3,
        out_specs=[SMEM] * 2,
        compiler_params=params(16),
    )(rows, cols, counts)


def load_kernel(values):
    def body(hbm, out, sem):
        copy = pltpu.make_async_copy(hbm, out, sem)
        copy.start()
        copy.wait()

    return pl.pallas_call(
        body,
        out_shape=jax.ShapeDtypeStruct(values.shape, values.dtype),
        in_specs=[pl.BlockSpec(memory_space=pltpu.HBM)],
        out_specs=VMEM,
        scratch_shapes=[pltpu.SemaphoreType.DMA],
        compiler_params=params(16),
    )(values)


def each_tile(k, list_ref, len_ref, step):
    def some(j, _):
        for u in range(UNROLL):
            e = list_ref[k, j * UNROLL + u]
            step(e & 255, (e >> 8) & 255, e >> 16)
        return 0

    lax.fori_loop(0, len_ref[k], some, 0)


def bases(sets):
    at, out = 0, []
    for k in sets:
        out.append(at)
        at += 2 * len(SETS[k]) + 1
    return out, at


def forward_kernel(sets, lists, lens, tiles, got, acc, last):
    blocks = [got[o] for k in sets for o in SETS[k]]
    n = len(blocks)
    width = blocks[0].shape[1]
    shape = (ROW_TILES + 1, TILE, width)
    starts, total = bases(sets)

    def body(list_ref, len_ref, a_ref, *refs):
        x_refs, rest = refs[:n], refs[n:]
        x_all = rest[-1]
        acc_ref = rest[-2]
        if acc is None:
            acc_ref[...] = jnp.zeros_like(acc_ref)
        else:
            acc_ref[...] = rest[0][...]
        x_iter = iter(x_refs)
        for k, start in zip(sets, starts):
            for i in range(len(SETS[k])):
                ref = next(x_iter)
                for t in range(2):
                    x_all[start + 2 * i + t] = ref[t * TILE : (t + 1) * TILE, :]
            x_all[start + 2 * len(SETS[k])] = jnp.zeros_like(x_all[0])
        for k, start in zip(sets, starts):

            def step(tile, near, place, start=start):
                acc_ref[place] += jnp.dot(a_ref[tile], x_all[start + near], preferred_element_type=F32)

            each_tile(k, list_ref, len_ref, step)
        if last:
            out_ref = rest[-3]
            for p in range(ROW_TILES):
                out_ref[p] = acc_ref[p].astype(BF16)

    ins = [lists, lens, tiles, *blocks] + ([] if acc is None else [acc])
    scratch = [pltpu.VMEM((total, TILE, width), BF16)]
    if last:
        out_shape = jax.ShapeDtypeStruct((ROW_TILES, TILE, width), BF16)
        scratch = [pltpu.VMEM(shape, F32)] + scratch
    else:
        out_shape = jax.ShapeDtypeStruct(shape, F32)
    return pl.pallas_call(
        body,
        out_shape=out_shape,
        in_specs=[SMEM] * 2 + [VMEM] * (len(ins) - 2),
        out_specs=VMEM,
        scratch_shapes=scratch,
        compiler_params=params(16),
        cost_estimate=pl.CostEstimate(
            flops=2 * n * 12 * TILE * TILE * width, bytes_accessed=n * 5 * TILE * TILE * 2, transcendentals=0
        ),
    )(*ins)


def backward_kernel(k, lists, lens, tiles, mine, theirs):
    n = len(SETS[k]) // 2
    width = mine.shape[1]

    def body(list_ref, len_ref, a_ref, mine_ref, their_ref, *refs):
        outs, other, (g_all, acc_ref) = refs[:n], refs[n], refs[n + 1 :]
        half = ROW_TILES // 2
        g_all[0:half] = mine_ref[...]
        g_all[half : 2 * half] = their_ref[...]
        g_all[2 * half] = jnp.zeros_like(g_all[2 * half])
        acc_ref[...] = jnp.zeros_like(acc_ref)

        def step(tile, near, place):
            acc_ref[near] += jnp.dot(g_all[place], a_ref[tile], preferred_element_type=F32)

        each_tile(k, list_ref, len_ref, step)
        for i in range(n):
            for t in range(2):
                outs[i][:, t * TILE : (t + 1) * TILE] = acc_ref[4 * i + t].astype(BF16)
                other[i, :, t * TILE : (t + 1) * TILE] = acc_ref[4 * i + 2 + t].astype(BF16)

    result = pl.pallas_call(
        body,
        out_shape=[jax.ShapeDtypeStruct((width, 2 * TILE), BF16)] * n
        + [jax.ShapeDtypeStruct((n, width, 2 * TILE), BF16)],
        in_specs=[SMEM] * 2 + [VMEM] * 3,
        out_specs=[VMEM] * (n + 1),
        scratch_shapes=[
            pltpu.VMEM((ROW_TILES + 1, width, TILE), BF16),
            pltpu.VMEM((4 * n + 1, width, TILE), F32),
        ],
        compiler_params=params(16),
        cost_estimate=pl.CostEstimate(
            flops=4 * n * 12 * TILE * TILE * width, bytes_accessed=n * 10 * TILE * TILE * 2, transcendentals=0
        ),
    )(lists, lens, tiles, mine, theirs)
    return result[:n], result[n]


def join_kernel(pieces):
    sizes = [p.shape[0] for p in pieces]

    def body(*refs):
        at = 0
        for ref, size in zip(refs, sizes):
            refs[-1][at : at + size] = ref[...]
            at += size

    return pl.pallas_call(
        body,
        out_shape=jax.ShapeDtypeStruct((sum(sizes),) + pieces[0].shape[1:], pieces[0].dtype),
        in_specs=[VMEM] * len(pieces),
        out_specs=VMEM,
        compiler_params=params(16),
    )(*pieces)


NT = (((1,), (1,)), ((), ()))
TN = (((0,), (0,)), ((), ()))


def dense_body(x_ref, a0_ref, a1_ref, cot_ref, ws_ref, wn_ref, bias_ref, out_ref, dz_ref, agg_ref, dagg_ref):
    agg = (a0_ref[...].astype(F32) + a1_ref[...].astype(F32)).astype(BF16)
    agg_ref[...] = agg
    z = (
        jnp.dot(x_ref[...], ws_ref[...], preferred_element_type=F32)
        + jnp.dot(agg, wn_ref[...], preferred_element_type=F32)
        + bias_ref[...]
    )
    sig = jax.nn.sigmoid(z)
    out_ref[...] = (z * sig).astype(BF16)
    dz = (cot_ref[...].astype(F32) * sig * (1.0 + z * (1.0 - sig))).astype(BF16)
    dz_ref[...] = dz
    dagg = lax.dot_general(wn_ref[...], dz, NT, preferred_element_type=F32).astype(BF16)
    for t in range(2):
        dagg_ref[t] = dagg[:, t * TILE : (t + 1) * TILE]


def dense_kernel(x, a0, a1, cot, w_self, w_neigh, bias):
    n, f = x.shape
    return pl.pallas_call(
        dense_body,
        out_shape=[jax.ShapeDtypeStruct((n, f), BF16)] * 3 + [jax.ShapeDtypeStruct((2, f, TILE), BF16)],
        in_specs=[VMEM] * 7,
        out_specs=[VMEM] * 4,
        compiler_params=params(16),
    )(x, a0, a1, cot, w_self, w_neigh, bias)


PART = 256 + 16


def weight_body(x_ref, agg_ref, dz_ref, ws_ref, parts_ref, own_ref):
    z, yl, yh, x, core = axes()
    dz = dz_ref[...]
    gb = jnp.sum(dz.astype(F32), axis=0, keepdims=True)
    bias = jnp.broadcast_to(gb, (16, gb.shape[1])).astype(BF16)
    for h, ref in enumerate((x_ref, agg_ref)):
        grad = lax.dot_general(ref[...], dz, TN, preferred_element_type=F32).astype(BF16)
        parts_ref[core ^ h, 0:256, :] = grad
        parts_ref[core ^ h, 256:PART, :] = bias
    own_ref[...] = lax.dot_general(dz, ws_ref[...], NT, preferred_element_type=F32)


def weight_kernel(x, agg, dz, w_self):
    n, f = x.shape
    return pl.pallas_call(
        weight_body,
        out_shape=[jax.ShapeDtypeStruct((2, PART, f), BF16), jax.ShapeDtypeStruct((n, f), F32)],
        in_specs=[VMEM] * 4,
        out_specs=[VMEM] * 2,
        compiler_params=params(16),
    )(x, agg, dz, w_self)


def hop_kernel(terms, moving, w):
    refs = [t[0] if isinstance(t, tuple) else t for t in terms]
    at = [t[1] if isinstance(t, tuple) else None for t in terms]
    rows, width = refs[0].shape[-2:]

    def body(*refs):
        out, rider = refs[-1], refs[-2]
        total = None
        for ref, i in zip(refs, at):
            term = (ref[...] if i is None else ref[i]).astype(F32)
            total = term if total is None else total + term
        if moving is None:
            out[rows:, :] = rider[...]
        else:
            total = total + rider[0:rows, :].astype(F32)
            out[rows:, :] = rider[rows:, :]
        out[0:rows, :] = total.astype(BF16)

    ins = refs + [w if moving is None else moving]
    return pl.pallas_call(
        body,
        out_shape=jax.ShapeDtypeStruct((rows + PART, width), BF16),
        in_specs=[VMEM] * len(ins),
        out_specs=VMEM,
        compiler_params=params(16),
    )(*ins)


def total_kernel(w, ups, downs):
    n = len(ups) + len(downs) + 1
    rows = ups[0].shape[0] - PART

    def body(*refs):
        out, all_ref = refs[-2:]
        z = axes()[0]
        all_ref[z] = refs[0][...]
        for j in range(len(ups)):
            all_ref[(z - 1 - j) & (NZ - 1)] = refs[1 + j][rows:, :]
        for j in range(len(downs)):
            all_ref[(z + 1 + j) & (NZ - 1)] = refs[1 + len(ups) + j][rows:, :]
        total = all_ref[0].astype(F32)
        for i in range(1, NZ):
            total = total + all_ref[i].astype(F32)
        out[...] = total.astype(BF16)

    return pl.pallas_call(
        body,
        out_shape=jax.ShapeDtypeStruct(w.shape, BF16),
        in_specs=[VMEM] * n,
        out_specs=VMEM,
        scratch_shapes=[pltpu.VMEM((NZ,) + w.shape, BF16)],
        compiler_params=params(16),
    )(w, *ups, *downs)


def final_body(own_ref, t_ref, up_ref, down_ref, y_ref, w0_ref, w1_ref, gf_ref, gs_ref, gn_ref, gb_ref):
    core = axes()[4]
    f = t_ref.shape[0]
    spread = (
        t_ref[...].astype(F32) + up_ref[0:f, :].astype(F32) + down_ref[0:f, :].astype(F32) + y_ref[...].astype(F32)
    )
    gf_ref[...] = (own_ref[...] + spread.T).astype(BF16)

    def write(first, second):
        gs_ref[...] = first[0:f, :].astype(F32)
        gn_ref[...] = second[0:f, :].astype(F32)
        gb_ref[...] = first[f:PART, :].astype(F32)[0:1]

    pl.when(core == 0)(lambda: write(w0_ref, w1_ref))
    pl.when(core == 1)(lambda: write(w1_ref, w0_ref))


def final_kernel(own, t, up, down, y, w0, w1):
    n, f = own.shape
    sq = jax.ShapeDtypeStruct((f, f), F32)
    return pl.pallas_call(
        final_body,
        out_shape=[jax.ShapeDtypeStruct((n, f), BF16), sq, sq, jax.ShapeDtypeStruct((1, f), F32)],
        in_specs=[VMEM] * 7,
        out_specs=[VMEM] * 4,
        compiler_params=params(16),
    )(own, t, up, down, y, w0, w1)


def add(*terms):
    total = terms[0].astype(F32)
    for t in terms[1:]:
        total = total + t.astype(F32)
    return total.astype(BF16)


def flip_z(value, bit):
    return permute(value, dz=lambda z: (z ^ bit) - z)


def after(value, *done):
    return lax.optimization_barrier((value, *done))[0]


def local(features, w_self, w_neigh, bias, cotangent, tile_values, tile_rows, tile_cols, tile_counts):
    width = features.shape[1]
    lists, lens = list_kernel(tile_rows[0, 0], tile_cols[0, 0], tile_counts[0, 0])
    tiles = load_kernel(tile_values.reshape((-1,) + tile_values.shape[4:]))

    together = lax.optimization_barrier
    up, down = permute(features, dz=1), permute(features, dz=-1)
    got = {(0, 0): features}
    up, down, got[0, 1], lists = together((up, down, permute(features, dyl=1), lists))
    acc = None
    for k in (1, 2, 3, 4):
        got[-k, 0], got[k, 0] = up, down
        here = (up, down)
        if k < 3:
            up, down = permute(up, dz=1), permute(down, dz=-1)
        elif k == 3:
            up = down = permute(up, dz=1)
        there = permute(join_kernel(here) if k < 4 else up, dyl=1)
        if k == 1:
            up, down, there, tiles = together((up, down, there, tiles))
        else:
            acc = forward_kernel((k - 2,), lists, lens, tiles, got, acc, False)
            up, down, there, acc = together((up, down, there, acc))
        rows = features.shape[0]
        got[-k, 1], got[k, 1] = (there[:rows], there[rows:]) if k < 4 else (there, there)
    partial = forward_kernel((3,), lists, lens, tiles, got, acc, True)

    partial = partial.reshape(2, 16 * TILE, width)
    half = add(partial[0], permute(partial[1], dc=1)).reshape(4, 4 * TILE, width)
    quarter = add(
        half[0], permute(half[1], dx=1), permute(half[3], dx=-1), permute(half[2], dx=2)
    ).reshape(2, 2 * TILE, width)
    other = permute(quarter[1], dyh=1)

    output, dz, agg, dagg = dense_kernel(
        features, quarter[0], other, cotangent, w_self, w_neigh, bias.reshape(1, width)
    )

    parts, own = weight_kernel(features, agg, dz, w_self)
    w = add(parts[0], permute(parts[1], dc=1))
    dagg_y, w = together((permute(dagg, dyh=1), w))
    pair = join_kernel([dagg, dagg_y])
    w = add(w, permute(w, dyl=1))
    from_left, from_right, w = together((permute(pair, dx=1), permute(pair, dx=-1), w))
    w = add(w, permute(w, dyh=1))
    left, right, w = together((permute(from_left[0:2], dx=1), permute(from_right[2:4], dx=-1), w))
    mine = join_kernel([pair, from_right, left, right, from_left])
    w = add(w, permute(w, dx=lambda x: (x ^ 1) - x))
    theirs, w = together((permute(mine, dc=1), w))

    def products(k):
        return backward_kernel(k, lists, lens, tiles, mine, theirs)

    (t4,), u4 = products(3)
    w, theirs, u4 = together((w, theirs, u4))
    (t3, t3d), u3 = products(2)
    y4, w, theirs, u3 = together(
        (permute(u4, dyl=1), add(w, permute(w, dx=lambda x: 3 - 2 * x)), theirs, u3)
    )
    (t2, t2d), u2 = products(1)
    up1, y3, theirs, u2 = together(
        (permute(hop_kernel([t4, (y4, 0)], None, w), dz=1), permute(u3, dyl=1), theirs, u2)
    )
    (t0, t1, t1d), u1 = products(0)
    up2, down1, y2, u1 = together(
        (
            permute(hop_kernel([t3, (y3, 0)], up1, w), dz=1),
            permute(hop_kernel([t3d, (y3, 1)], None, w), dz=-1),
            permute(u2, dyl=1),
            u1,
        )
    )
    up3, down2, y1 = together(
        (
            permute(hop_kernel([t2, (y2, 0)], up2, w), dz=1),
            permute(hop_kernel([t2d, (y2, 1)], down1, w), dz=-1),
            permute(u1[1:], dyl=1),
        )
    )
    up4, down3, y0 = together(
        (
            permute(hop_kernel([t1, (y1, 0)], up3, w), dz=1),
            permute(hop_kernel([t1d, (y1, 1)], down2, w), dz=-1),
            permute(u1[0], dyl=1),
        )
    )
    w = total_kernel(w, [up1, up2, up3, up4], [down1, down2, down3])
    grad_features, grad_self, grad_neigh, grad_bias = final_kernel(
        own, t0, up4, down3, y0, w, permute(w, dc=1)
    )
    return (output, grad_features, grad_self, grad_neigh, grad_bias.reshape(width))


def solution(mesh):
    in_specs = (
        P(("blk", "rep"), None),
        P(),
        P(),
        P(),
        P(("blk", "rep"), None),
        P("blk", "rep", None, None, None, None),
        P("blk", "rep", None, None),
        P("blk", "rep", None, None),
        P("blk", "rep", None),
    )
    out_specs = (P(("blk", "rep"), None), P(("blk", "rep"), None), P(), P(), P())
    return jax.shard_map(local, mesh=mesh, in_specs=in_specs, out_specs=out_specs, check_vma=False)
```

time: 697 us -> 162 us (0.23)
  waiting for transfers between devices: 316 us -> 70.7 us
  other arithmetic: 141 us -> 0.73 us
  local copies, waits for them, and re-layouts: 89.1 us -> 5.33 us
  blocking collectives: 77 us -> 0 us
  starting transfers between devices: 0.2 us -> 59.6 us
  matrix products: 52.5 us -> 0 us
  Pallas kernels: 0 us -> 21.3 us
  between operations: 13.8 us -> 1.09 us
    reduce_scatter x2 -> x0, waiting for transfers between devices: 149 us -> none  [the longest x1 76.9 us: local(): lax.psum_scatter(partial_value.astype(jnp.bfloat16), 'rep', scatter_dimen...]
    scatter-add x32 -> x0, other arithmetic: 132 us -> none  [the longest x16 66.1 us: column_one_block(): return acc.at[j * per_dev + cols_here].add(term)]
    all_gather x2 -> x0, waiting for transfers between devices: 117 us -> none  [the longest x1 74.2 us: local(): piece = lax.all_gather(features, 'blk', axis=0, tiled=True)]
    psum x1 -> x0, blocking collectives: 77 us -> none  [local(): lax.psum((jnp.einsum('nf,ng->fg', features, grad_z, preferred_element_typ...]
    ppermute x0 -> x41, waiting for transfers between devices: none -> 70.7 us  [permute(): return lax.ppermute(value, ('blk', 'rep'), pairs)]
    gather x32 -> x0, local copies, waits for them, and re-layouts: 70.1 us -> none  [the longest x16 35.1 us: column_one_block(): picked = jnp.take(grad_tiles, rows_here, axis=0)]
    ppermute x0 -> x41, starting transfers between devices: none -> 59.6 us  [permute(): return lax.ppermute(value, ('blk', 'rep'), pairs)]
    dot_general x38 -> x0, matrix products: 52.5 us -> none  [the longest x16 23 us: column_one_block(): jnp.einsum('sji,sjf->sif', vals, picked, preferred_element_type=jnp.float32)]
  transfers between devices with their start and end apart: 5 -> 41, of which waited for: 5 -> 24; matrix products, arithmetic and copies ran while one was open for 21% -> 1% of each run, Pallas kernels for 0% -> 10%
where the time goes in v1:
time: 162 us; the launch traced here: 159 us
  waiting for transfers between devices  70.7 us (44%)
  starting transfers between devices  59.6 us (37%)
  Pallas kernels  21.3 us (13%)
  local copies, waits for them, and re-layouts  5.33 us (3%)
    ppermute x41, waiting for transfers between devices, permute(): return lax.ppermute(value, ('blk', 'rep'), pairs)  70.7 us
    ppermute x41, starting transfers between devices, permute(): return lax.ppermute(value, ('blk', 'rep'), pairs)  59.6 us
    pallas_call x4, Pallas kernels, forward_kernel(): pl.pallas_call(body, out_shape=out_shape, in_specs=[SMEM] * 2 + [VMEM] *...  7.58 us
    pallas_call x4, Pallas kernels, backward_kernel(): pl.pallas_call(body, out_shape=[jax.ShapeDtypeStruct((width, 2 * TILE), B...  7.05 us
    unnamed x16, local copies, waits for them, and re-layouts  5 us
  transfers between devices with their start and end apart: 41, of which 24 were waited for; matrix products, arithmetic and copies ran while one was open for 1% of the time, Pallas kernels for 10%

profile of v1, /device:TPU:8, one launch (start us, length us, event | category | flops | bytes accessed | tf_op | source)
XLA Modules:
  0.0 158.7 jit_solution(18276790741454691903)
XLA Ops:
  2.9 4.1 %collective-permute-start.1 = (bf16[256,256]{1,0:T(8,128)(2,1)}, bf16[256,256]{1,0:T(8,128)(2,1)S(1)}, u32[]{:S(2)}, u32[]{:S(2)}) collective-permute-start(bf16[256,256]{1,0:T(8,128)(2,1)} %x_ref.3), channel_id=1, source_target_pairs={{0,224},{1,225},{2,226},{3,227},{4,228},{5,229},{6,230},{7,231},{8... | collective-permute-start | bytes 393224 | tf_op jit(solution)/shard_map/ppermute | solution.py:29
  9.2 3.1 %shard_map.128 = (s32[4,88]{1,0:T(4,128)S(1)}, s32[4]{0:T(128)S(1)}) custom-call(s32[16,12]{1,0:T(8,128)S(1)} %bitcast.18, s32[16,12]{1,0:T(8,128)S(1)} %bitcast.19, s32[16]{0:T(128)S(1)} %bitcast.21), custom_call_target="tpu_custom_call" | custom-call | tf_op jit(solution)/shard_map/pallas_call | solution.py:77
  15.1 3.2 %collective-permute-start.4 = (bf16[256,256]{1,0:T(8,128)(2,1)S(1)}, bf16[256,256]{1,0:T(8,128)(2,1)S(1)}, u32[]{:S(2)}, u32[]{:S(2)}) collective-permute-start(bf16[256,256]{1,0:T(8,128)(2,1)S(1)} %collective-permute-done.1.refs_1_.refs_2_), channel_id=1, source_target_pairs={{0,224},{1,225},{2,226},{3,227},{4,228},{5,229},{6,230},{7,231},{8... | collective-permute-start | bytes 393224 | tf_op jit(solution)/shard_map/ppermute | solution.py:29
  18.3 2.8 %copy-done = bf16[1,1,16,12,128,128]{5,4,3,2,1,0:T(8,128)(2,1)S(1)} copy-done((bf16[1,1,16,12,128,128]{5,4,3,2,1,0:T(8,128)(2,1)S(1)}, bf16[1,1,16,12,128,128]{5,4,3,2,1,0:T(8,128)(2,1)}, u32[]{:S(2)}) %copy-start) | copy-done | bytes 6291480
  21.7 3.2 %collective-permute-start.7 = (bf16[256,256]{1,0:T(8,128)(2,1)S(1)}, bf16[256,256]{1,0:T(8,128)(2,1)S(1)}, u32[]{:S(2)}, u32[]{:S(2)}) collective-permute-start(bf16[256,256]{1,0:T(8,128)(2,1)S(1)} %collective-permute-done.4.refs_1_.refs_0_), channel_id=1, source_target_pairs={{0,224},{1,225},{2,226},{3,227},{4,228},{5,229},{6,230},{7,231},{8... | collective-permute-start | bytes 393224 | tf_op jit(solution)/shard_map/ppermute | solution.py:29
  27.9 4.9 %collective-permute-done.8 = bf16[512,256]{1,0:T(8,128)(2,1)S(1)} collective-permute-done((bf16[512,256]{1,0:T(8,128)(2,1)S(1)}, bf16[512,256]{1,0:T(8,128)(2,1)S(1)}, u32[]{:S(2)}, u32[]{:S(2)}) %collective-permute-start.8) | collective-permute-done | bytes 262176 | tf_op jit(solution)/shard_map/ppermute | solution.py:29
  35.1 3.8 %collective-permute-done.9.refs_0_ = bf16[256,256]{1,0:T(8,128)(2,1)S(1)} collective-permute-done((bf16[256,256]{1,0:T(8,128)(2,1)S(1)}, bf16[256,256]{1,0:T(8,128)(2,1)S(1)}, u32[]{:S(2)}, u32[]{:S(2)}) %collective-permute-start.9) | collective-permute-done | bytes 131104 | tf_op jit(solution)/shard_map/ppermute | solution.py:29
  52.3 2.7 %collective-permute-start.15 = (bf16[512,256]{1,0:T(8,128)(2,1)S(1)}, bf16[512,256]{1,0:T(8,128)(2,1)S(1)}, u32[]{:S(2)}, u32[]{:S(2)}) collective-permute-start(bf16[512,256]{1,0:T(8,128)(2,1)S(1)} %get-tuple-element.154), channel_id=1, source_target_pairs={{0,4},{1,5},{2,6},{3,7},{4,0},{5,1},{6,2},{7,3},{8,12},{9,13},{10,... | collective-permute-start | bytes 786440 | tf_op jit(solution)/shard_map/ppermute | solution.py:29
  56.5 3.9 %collective-permute-done.13 = bf16[512,256]{1,0:T(8,128)(2,1)S(1)} collective-permute-done((bf16[512,256]{1,0:T(8,128)(2,1)S(1)}, bf16[512,256]{1,0:T(8,128)(2,1)S(1)}, u32[]{:S(2)}, u32[]{:S(2)}) %collective-permute-start.13) | collective-permute-done | bytes 262176 | tf_op jit(solution)/shard_map/ppermute | solution.py:29
  60.4 6.6 %collective-permute-done.15 = bf16[512,256]{1,0:T(8,128)(2,1)S(1)} collective-permute-done((bf16[512,256]{1,0:T(8,128)(2,1)S(1)}, bf16[512,256]{1,0:T(8,128)(2,1)S(1)}, u32[]{:S(2)}, u32[]{:S(2)}) %collective-permute-start.15) | collective-permute-done | bytes 262176 | tf_op jit(solution)/shard_map/ppermute | solution.py:29
  69.5 4.2 %collective-permute-done.16.a1_ref = bf16[256,256]{1,0:T(8,128)(2,1)S(1)} collective-permute-done((bf16[256,256]{1,0:T(8,128)(2,1)S(1)}, bf16[256,256]{1,0:T(8,128)(2,1)S(1)}, u32[]{:S(2)}, u32[]{:S(2)}) %collective-permute-start.16) | collective-permute-done | bytes 131104 | tf_op jit(solution)/shard_map/ppermute | solution.py:29
  77.6 5.0 %collective-permute-done.17.refs_1_ = bf16[2,256,128]{2,1,0:T(8,128)(2,1)S(1)} collective-permute-done((bf16[2,256,128]{2,1,0:T(8,128)(2,1)S(1)}, bf16[2,256,128]{2,1,0:T(8,128)(2,1)S(1)}, u32[]{:S(2)}, u32[]{:S(2)}) %collective-permute-start.17) | collective-permute-done | bytes 131104 | tf_op jit(solution)/shard_map/ppermute | solution.py:29
  83.1 2.8 %collective-permute-start.20 = (bf16[4,256,128]{2,1,0:T(8,128)(2,1)S(1)}, bf16[4,256,128]{2,1,0:T(8,128)(2,1)S(1)}, u32[]{:S(2)}, u32[]{:S(2)}) collective-permute-start(bf16[4,256,128]{2,1,0:T(8,128)(2,1)S(1)} %shard_map.139.refs_0_), channel_id=1, source_target_pairs={{0,6},{1,7},{2,0},{3,1},{4,2},{5,3},{6,4},{7,5},{8,14},{9,15},{10,... | collective-permute-start | bytes 786440 | tf_op jit(solution)/shard_map/ppermute | solution.py:29
  87.8 3.1 %collective-permute-done.20.refs_1_ = bf16[4,256,128]{2,1,0:T(8,128)(2,1)S(1)} collective-permute-done((bf16[4,256,128]{2,1,0:T(8,128)(2,1)S(1)}, bf16[4,256,128]{2,1,0:T(8,128)(2,1)S(1)}, u32[]{:S(2)}, u32[]{:S(2)}) %collective-permute-start.20) | collective-permute-done | bytes 262176 | tf_op jit(solution)/shard_map/ppermute | solution.py:29
  90.9 3.4 %collective-permute-done.19.refs_4_ = bf16[4,256,128]{2,1,0:T(8,128)(2,1)S(1)} collective-permute-done((bf16[4,256,128]{2,1,0:T(8,128)(2,1)S(1)}, bf16[4,256,128]{2,1,0:T(8,128)(2,1)S(1)}, u32[]{:S(2)}, u32[]{:S(2)}) %collective-permute-start.19) | collective-permute-done | bytes 262176 | tf_op jit(solution)/shard_map/ppermute | solution.py:29
  97.0 3.2 %collective-permute-start.23 = (bf16[2,256,128]{2,1,0:T(8,128)(2,1)S(1)}, bf16[2,256,128]{2,1,0:T(8,128)(2,1)S(1)}, u32[]{:S(2)}, u32[]{:S(2)}) collective-permute-start(bf16[2,256,128]{2,1,0:T(8,128)(2,1)S(1)} %slice.85), channel_id=1, source_target_pairs={{0,6},{1,7},{2,0},{3,1},{4,2},{5,3},{6,4},{7,5},{8,14},{9,15},{10,... | collective-permute-start | bytes 393224 | tf_op jit(solution)/shard_map/ppermute | solution.py:29
  103.4 6.0 %collective-permute-done.26 = bf16[272,256]{1,0:T(8,128)(2,1)S(1)} collective-permute-done((bf16[272,256]{1,0:T(8,128)(2,1)S(1)}, bf16[272,256]{1,0:T(8,128)(2,1)S(1)}, u32[]{:S(2)}, u32[]{:S(2)}) %collective-permute-start.26) | collective-permute-done | bytes 139296 | tf_op jit(solution)/shard_map/ppermute | solution.py:29
  110.7 3.5 %collective-permute-start.28 = (bf16[272,256]{1,0:T(8,128)(2,1)S(1)}, bf16[272,256]{1,0:T(8,128)(2,1)S(1)}, u32[]{:S(2)}, u32[]{:S(2)}) collective-permute-start(bf16[272,256]{1,0:T(8,128)(2,1)S(1)} %add_convert_fusion.2), channel_id=1, source_target_pairs={{0,6},{1,7},{2,4},{3,5},{4,2},{5,3},{6,0},{7,1},{8,14},{9,15},{10,... | collective-permute-start | bytes 417800 | tf_op jit(solution)/shard_map/ppermute | solution.py:29
  123.2 3.2 %collective-permute-done.30.refs_1_ = bf16[2,256,256]{2,1,0:T(8,128)(2,1)S(1)} collective-permute-done((bf16[2,256,256]{2,1,0:T(8,128)(2,1)S(1)}, bf16[2,256,256]{2,1,0:T(8,128)(2,1)S(1)}, u32[]{:S(2)}, u32[]{:S(2)}) %collective-permute-start.30) | collective-permute-done | bytes 262176 | tf_op jit(solution)/shard_map/ppermute | solution.py:29
  127.8 3.2 %collective-permute-start.32 = (bf16[528,256]{1,0:T(8,128)(2,1)S(1)}, bf16[528,256]{1,0:T(8,128)(2,1)S(1)}, u32[]{:S(2)}, u32[]{:S(2)}) collective-permute-start(bf16[528,256]{1,0:T(8,128)(2,1)S(1)} %shard_map.147), channel_id=1, source_target_pairs={{0,224},{1,225},{2,226},{3,227},{4,228},{5,229},{6,230},{7,231},{8... | collective-permute-start | bytes 811016 | tf_op jit(solution)/shard_map/ppermute | solution.py:29
  137.6 3.3 %collective-permute-start.35 = (bf16[528,256]{1,0:T(8,128)(2,1)S(1)}, bf16[528,256]{1,0:T(8,128)(2,1)S(1)}, u32[]{:S(2)}, u32[]{:S(2)}) collective-permute-start(bf16[528,256]{1,0:T(8,128)(2,1)S(1)} %shard_map.149), channel_id=1, source_target_pairs={{0,224},{1,225},{2,226},{3,227},{4,228},{5,229},{6,230},{7,231},{8... | collective-permute-start | bytes 811016 | tf_op jit(solution)/shard_map/ppermute | solution.py:29
  142.9 4.5 %collective-permute-done.36.refs_1_ = bf16[2,256,256]{2,1,0:T(8,128)(2,1)S(1)} collective-permute-done((bf16[2,256,256]{2,1,0:T(8,128)(2,1)S(1)}, bf16[2,256,256]{2,1,0:T(8,128)(2,1)S(1)}, u32[]{:S(2)}, u32[]{:S(2)}) %collective-permute-start.36) | collective-permute-done | bytes 262176 | tf_op jit(solution)/shard_map/ppermute | solution.py:29
  147.6 3.3 %collective-permute-start.38 = (bf16[528,256]{1,0:T(8,128)(2,1)S(1)}, bf16[528,256]{1,0:T(8,128)(2,1)S(1)}, u32[]{:S(2)}, u32[]{:S(2)}) collective-permute-start(bf16[528,256]{1,0:T(8,128)(2,1)S(1)} %shard_map.151), channel_id=1, source_target_pairs={{0,224},{1,225},{2,226},{3,227},{4,228},{5,229},{6,230},{7,231},{8... | collective-permute-start | bytes 811016 | tf_op jit(solution)/shard_map/ppermute | solution.py:29
  152.9 3.1 %collective-permute-done.39.y_ref = bf16[256,256]{1,0:T(8,128)(2,1)S(1)} collective-permute-done((bf16[256,256]{1,0:T(8,128)(2,1)S(1)}, bf16[256,256]{1,0:T(8,128)(2,1)S(1)}, u32[]{:S(2)}, u32[]{:S(2)}) %collective-permute-start.39) | collective-permute-done | bytes 131104 | tf_op jit(solution)/shard_map/ppermute | solution.py:29
  (118 shorter events, 67.4 us)
Async XLA Ops:
  0.6 11.7 %collective-permute-start.2 = (bf16[256,256]{1,0:T(8,128)(2,1)}, bf16[256,256]{1,0:T(8,128)(2,1)S(1)}, u32[]{:S(2)}, u32[]{:S(2)}) collective-permute-start(bf16[256,256]{1,0:T(8,128)(2,1)} %x_ref.3), channel_id=1, source_target_pairs={{0,16},{1,17},{2,18},{3,19},{4,20},{5,21},{6,22},{7,23},{8,24},{9,... | collective-permute-start | bytes 393224 | tf_op jit(solution)/shard_map/ppermute | solution.py:29
  2.9 9.4 %collective-permute-start.1 = (bf16[256,256]{1,0:T(8,128)(2,1)}, bf16[256,256]{1,0:T(8,128)(2,1)S(1)}, u32[]{:S(2)}, u32[]{:S(2)}) collective-permute-start(bf16[256,256]{1,0:T(8,128)(2,1)} %x_ref.3), channel_id=1, source_target_pairs={{0,224},{1,225},{2,226},{3,227},{4,228},{5,229},{6,230},{7,231},{8... | collective-permute-start | bytes 393224 | tf_op jit(solution)/shard_map/ppermute | solution.py:29
  13.4 8.1 %collective-permute-start.5 = (bf16[512,256]{1,0:T(8,128)(2,1)S(1)}, bf16[512,256]{1,0:T(8,128)(2,1)S(1)}, u32[]{:S(2)}, u32[]{:S(2)}) collective-permute-start(bf16[512,256]{1,0:T(8,128)(2,1)S(1)} %shard_map.129), channel_id=1, source_target_pairs={{0,16},{1,17},{2,18},{3,19},{4,20},{5,21},{6,22},{7,23},{8,24},{9,... | collective-permute-start | bytes 786440 | tf_op jit(solution)/shard_map/ppermute | solution.py:29
  15.1 6.5 %collective-permute-start.3 = (bf16[256,256]{1,0:T(8,128)(2,1)S(1)}, bf16[256,256]{1,0:T(8,128)(2,1)S(1)}, u32[]{:S(2)}, u32[]{:S(2)}) collective-permute-start(bf16[256,256]{1,0:T(8,128)(2,1)S(1)} %collective-permute-done.refs_0_.refs_4_), channel_id=1, source_target_pairs={{0,32},{1,33},{2,34},{3,35},{4,36},{5,37},{6,38},{7,39},{8,40},{9,... | collective-permute-start | bytes 393224 | tf_op jit(solution)/shard_map/ppermute | solution.py:29
  15.1 6.5 %collective-permute-start.4 = (bf16[256,256]{1,0:T(8,128)(2,1)S(1)}, bf16[256,256]{1,0:T(8,128)(2,1)S(1)}, u32[]{:S(2)}, u32[]{:S(2)}) collective-permute-start(bf16[256,256]{1,0:T(8,128)(2,1)S(1)} %collective-permute-done.1.refs_1_.refs_2_), channel_id=1, source_target_pairs={{0,224},{1,225},{2,226},{3,227},{4,228},{5,229},{6,230},{7,231},{8... | collective-permute-start | bytes 393224 | tf_op jit(solution)/shard_map/ppermute | solution.py:29
  24.9 7.8 %collective-permute-start.8 = (bf16[512,256]{1,0:T(8,128)(2,1)S(1)}, bf16[512,256]{1,0:T(8,128)(2,1)S(1)}, u32[]{:S(2)}, u32[]{:S(2)}) collective-permute-start(bf16[512,256]{1,0:T(8,128)(2,1)S(1)} %shard_map.131), channel_id=1, source_target_pairs={{0,16},{1,17},{2,18},{3,19},{4,20},{5,21},{6,22},{7,23},{8,24},{9,... | collective-permute-start | bytes 786440 | tf_op jit(solution)/shard_map/ppermute | solution.py:29
  32.8 7.9 %collective-permute-start.10 = (bf16[512,256]{1,0:T(8,128)(2,1)S(1)}, bf16[512,256]{1,0:T(8,128)(2,1)S(1)}, u32[]{:S(2)}, u32[]{:S(2)}) collective-permute-start(bf16[512,256]{1,0:T(8,128)(2,1)S(1)} %shard_map.133), channel_id=1, source_target_pairs={{0,16},{1,17},{2,18},{3,19},{4,20},{5,21},{6,22},{7,23},{8,24},{9,... | collective-permute-start | bytes 786440 | tf_op jit(solution)/shard_map/ppermute | solution.py:29
  50.7 9.6 %collective-permute-start.13 = (bf16[512,256]{1,0:T(8,128)(2,1)S(1)}, bf16[512,256]{1,0:T(8,128)(2,1)S(1)}, u32[]{:S(2)}, u32[]{:S(2)}) collective-permute-start(bf16[512,256]{1,0:T(8,128)(2,1)S(1)} %get-tuple-element.153), channel_id=1, source_target_pairs={{0,2},{1,3},{2,4},{3,5},{4,6},{5,7},{6,0},{7,1},{8,10},{9,11},{10,... | collective-permute-start | bytes 786440 | tf_op jit(solution)/shard_map/ppermute | solution.py:29
  52.3 14.7 %collective-permute-start.15 = (bf16[512,256]{1,0:T(8,128)(2,1)S(1)}, bf16[512,256]{1,0:T(8,128)(2,1)S(1)}, u32[]{:S(2)}, u32[]{:S(2)}) collective-permute-start(bf16[512,256]{1,0:T(8,128)(2,1)S(1)} %get-tuple-element.154), channel_id=1, source_target_pairs={{0,4},{1,5},{2,6},{3,7},{4,0},{5,1},{6,2},{7,3},{8,12},{9,13},{10,... | collective-permute-start | bytes 786440 | tf_op jit(solution)/shard_map/ppermute | solution.py:29
  55.0 11.9 %collective-permute-start.14 = (bf16[512,256]{1,0:T(8,128)(2,1)S(1)}, bf16[512,256]{1,0:T(8,128)(2,1)S(1)}, u32[]{:S(2)}, u32[]{:S(2)}) collective-permute-start(bf16[512,256]{1,0:T(8,128)(2,1)S(1)} %get-tuple-element.155), channel_id=1, source_target_pairs={{0,6},{1,7},{2,0},{3,1},{4,2},{5,3},{6,4},{7,5},{8,14},{9,15},{10,... | collective-permute-start | bytes 786440 | tf_op jit(solution)/shard_map/ppermute | solution.py:29
  67.2 6.6 %collective-permute-start.16 = (bf16[256,256]{1,0:T(8,128)(2,1)S(1)}, bf16[256,256]{1,0:T(8,128)(2,1)S(1)}, u32[]{:S(2)}, u32[]{:S(2)}) collective-permute-start(bf16[256,256]{1,0:T(8,128)(2,1)S(1)} %get-tuple-element.156), channel_id=1, source_target_pairs={{0,8},{1,9},{2,10},{3,11},{4,12},{5,13},{6,14},{7,15},{8,0},{9,1},... | collective-permute-start | bytes 393224 | tf_op jit(solution)/shard_map/ppermute | solution.py:29
  75.2 7.4 %collective-permute-start.17 = (bf16[2,256,128]{2,1,0:T(8,128)(2,1)S(1)}, bf16[2,256,128]{2,1,0:T(8,128)(2,1)S(1)}, u32[]{:S(2)}, u32[]{:S(2)}) collective-permute-start(bf16[2,256,128]{2,1,0:T(8,128)(2,1)S(1)} %get-tuple-element.102.refs_0_), channel_id=1, source_target_pairs={{0,8},{1,9},{2,10},{3,11},{4,12},{5,13},{6,14},{7,15},{8,0},{9,1},... | collective-permute-start | bytes 393224 | tf_op jit(solution)/shard_map/ppermute | solution.py:29
  83.1 7.9 %collective-permute-start.20 = (bf16[4,256,128]{2,1,0:T(8,128)(2,1)S(1)}, bf16[4,256,128]{2,1,0:T(8,128)(2,1)S(1)}, u32[]{:S(2)}, u32[]{:S(2)}) collective-permute-start(bf16[4,256,128]{2,1,0:T(8,128)(2,1)S(1)} %shard_map.139.refs_0_), channel_id=1, source_target_pairs={{0,6},{1,7},{2,0},{3,1},{4,2},{5,3},{6,4},{7,5},{8,14},{9,15},{10,... | collective-permute-start | bytes 786440 | tf_op jit(solution)/shard_map/ppermute | solution.py:29
  85.9 8.5 %collective-permute-start.19 = (bf16[4,256,128]{2,1,0:T(8,128)(2,1)S(1)}, bf16[4,256,128]{2,1,0:T(8,128)(2,1)S(1)}, u32[]{:S(2)}, u32[]{:S(2)}) collective-permute-start(bf16[4,256,128]{2,1,0:T(8,128)(2,1)S(1)} %shard_map.139.refs_0_), channel_id=1, source_target_pairs={{0,2},{1,3},{2,4},{3,5},{4,6},{5,7},{6,0},{7,1},{8,10},{9,11},{10,... | collective-permute-start | bytes 786440 | tf_op jit(solution)/shard_map/ppermute | solution.py:29
  94.4 6.6 %collective-permute-start.24 = (bf16[272,256]{1,0:T(8,128)(2,1)S(1)}, bf16[272,256]{1,0:T(8,128)(2,1)S(1)}, u32[]{:S(2)}, u32[]{:S(2)}) collective-permute-start(bf16[272,256]{1,0:T(8,128)(2,1)S(1)} %add_convert_fusion.4), channel_id=1, source_target_pairs={{0,8},{1,9},{2,10},{3,11},{4,12},{5,13},{6,14},{7,15},{8,0},{9,1},... | collective-permute-start | bytes 417800 | tf_op jit(solution)/shard_map/ppermute | solution.py:29
  110.7 7.3 %collective-permute-start.28 = (bf16[272,256]{1,0:T(8,128)(2,1)S(1)}, bf16[272,256]{1,0:T(8,128)(2,1)S(1)}, u32[]{:S(2)}, u32[]{:S(2)}) collective-permute-start(bf16[272,256]{1,0:T(8,128)(2,1)S(1)} %add_convert_fusion.2), channel_id=1, source_target_pairs={{0,6},{1,7},{2,4},{3,5},{4,2},{5,3},{6,0},{7,1},{8,14},{9,15},{10,... | collective-permute-start | bytes 417800 | tf_op jit(solution)/shard_map/ppermute | solution.py:29
  119.3 8.3 %collective-permute-start.29 = (bf16[528,256]{1,0:T(8,128)(2,1)S(1)}, bf16[528,256]{1,0:T(8,128)(2,1)S(1)}, u32[]{:S(2)}, u32[]{:S(2)}) collective-permute-start(bf16[528,256]{1,0:T(8,128)(2,1)S(1)} %shard_map.143), channel_id=1, source_target_pairs={{0,32},{1,33},{2,34},{3,35},{4,36},{5,37},{6,38},{7,39},{8,40},{9,... | collective-permute-start | bytes 811016 | tf_op jit(solution)/shard_map/ppermute | solution.py:29
  119.4 7.0 %collective-permute-start.30 = (bf16[2,256,256]{2,1,0:T(8,128)(2,1)S(1)}, bf16[2,256,256]{2,1,0:T(8,128)(2,1)S(1)}, u32[]{:S(2)}, u32[]{:S(2)}) collective-permute-start(bf16[2,256,256]{2,1,0:T(8,128)(2,1)S(1)} %get-tuple-element.122), channel_id=1, source_target_pairs={{0,16},{1,17},{2,18},{3,19},{4,20},{5,21},{6,22},{7,23},{8,24},{9,... | collective-permute-start | bytes 786440 | tf_op jit(solution)/shard_map/ppermute | solution.py:29
  127.7 9.7 %collective-permute-start.31 = (bf16[528,256]{1,0:T(8,128)(2,1)S(1)}, bf16[528,256]{1,0:T(8,128)(2,1)S(1)}, u32[]{:S(2)}, u32[]{:S(2)}) collective-permute-start(bf16[528,256]{1,0:T(8,128)(2,1)S(1)} %shard_map.146), channel_id=1, source_target_pairs={{0,32},{1,33},{2,34},{3,35},{4,36},{5,37},{6,38},{7,39},{8,40},{9,... | collective-permute-start | bytes 811016 | tf_op jit(solution)/shard_map/ppermute | solution.py:29
  127.8 9.6 %collective-permute-start.32 = (bf16[528,256]{1,0:T(8,128)(2,1)S(1)}, bf16[528,256]{1,0:T(8,128)(2,1)S(1)}, u32[]{:S(2)}, u32[]{:S(2)}) collective-permute-start(bf16[528,256]{1,0:T(8,128)(2,1)S(1)} %shard_map.147), channel_id=1, source_target_pairs={{0,224},{1,225},{2,226},{3,227},{4,228},{5,229},{6,230},{7,231},{8... | collective-permute-start | bytes 811016 | tf_op jit(solution)/shard_map/ppermute | solution.py:29
  137.4 9.9 %collective-permute-start.34 = (bf16[528,256]{1,0:T(8,128)(2,1)S(1)}, bf16[528,256]{1,0:T(8,128)(2,1)S(1)}, u32[]{:S(2)}, u32[]{:S(2)}) collective-permute-start(bf16[528,256]{1,0:T(8,128)(2,1)S(1)} %shard_map.148), channel_id=1, source_target_pairs={{0,32},{1,33},{2,34},{3,35},{4,36},{5,37},{6,38},{7,39},{8,40},{9,... | collective-permute-start | bytes 811016 | tf_op jit(solution)/shard_map/ppermute | solution.py:29
  137.6 9.8 %collective-permute-start.35 = (bf16[528,256]{1,0:T(8,128)(2,1)S(1)}, bf16[528,256]{1,0:T(8,128)(2,1)S(1)}, u32[]{:S(2)}, u32[]{:S(2)}) collective-permute-start(bf16[528,256]{1,0:T(8,128)(2,1)S(1)} %shard_map.149), channel_id=1, source_target_pairs={{0,224},{1,225},{2,226},{3,227},{4,228},{5,229},{6,230},{7,231},{8... | collective-permute-start | bytes 811016 | tf_op jit(solution)/shard_map/ppermute | solution.py:29
  147.4 8.5 %collective-permute-start.37 = (bf16[528,256]{1,0:T(8,128)(2,1)S(1)}, bf16[528,256]{1,0:T(8,128)(2,1)S(1)}, u32[]{:S(2)}, u32[]{:S(2)}) collective-permute-start(bf16[528,256]{1,0:T(8,128)(2,1)S(1)} %shard_map.150), channel_id=1, source_target_pairs={{0,32},{1,33},{2,34},{3,35},{4,36},{5,37},{6,38},{7,39},{8,40},{9,... | collective-permute-start | bytes 811016 | tf_op jit(solution)/shard_map/ppermute | solution.py:29
  147.6 8.4 %collective-permute-start.38 = (bf16[528,256]{1,0:T(8,128)(2,1)S(1)}, bf16[528,256]{1,0:T(8,128)(2,1)S(1)}, u32[]{:S(2)}, u32[]{:S(2)}) collective-permute-start(bf16[528,256]{1,0:T(8,128)(2,1)S(1)} %shard_map.151), channel_id=1, source_target_pairs={{0,224},{1,225},{2,226},{3,227},{4,228},{5,229},{6,230},{7,231},{8... | collective-permute-start | bytes 811016 | tf_op jit(solution)/shard_map/ppermute | solution.py:29
  (24 other events, 202.2 us)

commit v2 on v1

--- a/solution.py
+++ b/solution.py
@@ -51,18 +51,17 @@
 
 def list_body(rows_ref, cols_ref, cnt_ref, list_ref, len_ref):
     z, yl, yh, x, core = axes()
-    slots = rows_ref.shape[1]
+    slots = rows_ref.shape[0]
     for k, offsets in enumerate(SETS):
         n = jnp.int32(0)
         for i, (dz, dy) in enumerate(offsets):
             c = ((z + dz + NZ) & (NZ - 1)) * 2 + (yl ^ dy)
 
             def put(s, _, c=c, i=i, k=k, n=n):
-                row = rows_ref[c, s]
+                row = rows_ref[s, c]
                 q = row >> 1
-                place = (((q & 1) ^ core) * 4 + (((q >> 1) - x) & 3)) * 2 + ((q >> 3) ^ yh)
-                place = place * 2 + (row & 1)
-                near = i * 2 + cols_ref[c, s]
+                place = ((q & 1) ^ core) * 16 + (q >> 1) * 2 + (row & 1)
+                near = i * 2 + cols_ref[s, c]
                 list_ref[k, n + s] = (c * slots + s) | (near << 8) | (place << 16)
                 return 0
 
@@ -175,13 +174,14 @@
 
 def backward_kernel(k, lists, lens, tiles, mine, theirs):
     n = len(SETS[k]) // 2
-    width = mine.shape[1]
+    width = (mine.shape[0] - 2 * PART) * 2 // ROW_TILES
 
     def body(list_ref, len_ref, a_ref, mine_ref, their_ref, *refs):
         outs, other, (g_all, acc_ref) = refs[:n], refs[n], refs[n + 1 :]
         half = ROW_TILES // 2
-        g_all[0:half] = mine_ref[...]
-        g_all[half : 2 * half] = their_ref[...]
+        for i in range(half):
+            g_all[i] = mine_ref[i * width : (i + 1) * width, :]
+            g_all[half + i] = their_ref[i * width : (i + 1) * width, :]
         g_all[2 * half] = jnp.zeros_like(g_all[2 * half])
         acc_ref[...] = jnp.zeros_like(acc_ref)
 
@@ -234,9 +234,14 @@
 TN = (((0,), (0,)), ((), ()))
 
 
-def dense_body(x_ref, a0_ref, a1_ref, cot_ref, ws_ref, wn_ref, bias_ref, out_ref, dz_ref, agg_ref, dagg_ref):
-    agg = (a0_ref[...].astype(F32) + a1_ref[...].astype(F32)).astype(BF16)
-    agg_ref[...] = agg
+PART = 64 + 16
+
+
+def dense_body(x_ref, parts_ref, cot_ref, ws_ref, wn_ref, bias_ref, out_ref, own_ref, send_ref):
+    agg = parts_ref[0].astype(F32)
+    for i in range(1, parts_ref.shape[0]):
+        agg = agg + parts_ref[i].astype(F32)
+    agg = agg.astype(BF16)
     z = (
         jnp.dot(x_ref[...], ws_ref[...], preferred_element_type=F32)
         + jnp.dot(agg, wn_ref[...], preferred_element_type=F32)
@@ -245,71 +250,101 @@
     sig = jax.nn.sigmoid(z)
     out_ref[...] = (z * sig).astype(BF16)
     dz = (cot_ref[...].astype(F32) * sig * (1.0 + z * (1.0 - sig))).astype(BF16)
-    dz_ref[...] = dz
+    own_ref[...] = lax.dot_general(dz, ws_ref[...], NT, preferred_element_type=F32)
     dagg = lax.dot_general(wn_ref[...], dz, NT, preferred_element_type=F32).astype(BF16)
-    for t in range(2):
-        dagg_ref[t] = dagg[:, t * TILE : (t + 1) * TILE]
-
-
-def dense_kernel(x, a0, a1, cot, w_self, w_neigh, bias):
+    grads = [
+        lax.dot_general(left, dz, TN, preferred_element_type=F32).astype(BF16) for left in (x_ref[...], agg)
+    ]
+    total = jnp.sum(dz.astype(F32), axis=0, keepdims=True)
+    total = jnp.broadcast_to(total, (16, total.shape[1])).astype(BF16)
+    f = dagg.shape[0]
+    for d in range(8):
+        part = grads[d // 4][(d % 4) * 64 : (d % 4 + 1) * 64]
+        for t in range(2):
+            half = slice(t * TILE, (t + 1) * TILE)
+            send_ref[d, t * f : (t + 1) * f, :] = dagg[:, half]
+            send_ref[d, 2 * f + t * 64 : 2 * f + (t + 1) * 64, :] = part[:, half]
+            send_ref[d, 2 * f + 128 + t * 16 : 2 * f + 128 + (t + 1) * 16, :] = total[:, half]
+
+
+def dense_kernel(x, parts, cot, w_self, w_neigh, bias):
     n, f = x.shape
     return pl.pallas_call(
         dense_body,
-        out_shape=[jax.ShapeDtypeStruct((n, f), BF16)] * 3 + [jax.ShapeDtypeStruct((2, f, TILE), BF16)],
-        in_specs=[VMEM] * 7,
-        out_specs=[VMEM] * 4,
-        compiler_params=params(16),
-    )(x, a0, a1, cot, w_self, w_neigh, bias)
-
-
-PART = 256 + 16
-
-
-def weight_body(x_ref, agg_ref, dz_ref, ws_ref, parts_ref, own_ref):
-    z, yl, yh, x, core = axes()
-    dz = dz_ref[...]
-    gb = jnp.sum(dz.astype(F32), axis=0, keepdims=True)
-    bias = jnp.broadcast_to(gb, (16, gb.shape[1])).astype(BF16)
-    for h, ref in enumerate((x_ref, agg_ref)):
-        grad = lax.dot_general(ref[...], dz, TN, preferred_element_type=F32).astype(BF16)
-        parts_ref[core ^ h, 0:256, :] = grad
-        parts_ref[core ^ h, 256:PART, :] = bias
-    own_ref[...] = lax.dot_general(dz, ws_ref[...], NT, preferred_element_type=F32)
-
-
-def weight_kernel(x, agg, dz, w_self):
-    n, f = x.shape
-    return pl.pallas_call(
-        weight_body,
-        out_shape=[jax.ShapeDtypeStruct((2, PART, f), BF16), jax.ShapeDtypeStruct((n, f), F32)],
-        in_specs=[VMEM] * 4,
-        out_specs=[VMEM] * 2,
-        compiler_params=params(16),
-    )(x, agg, dz, w_self)
+        out_shape=[
+            jax.ShapeDtypeStruct((n, f), BF16),
+            jax.ShapeDtypeStruct((n, f), F32),
+            jax.ShapeDtypeStruct((8, 2 * f + 2 * PART, TILE), BF16),
+        ],
+        in_specs=[VMEM] * 6,
+        out_specs=[VMEM] * 3,
+        compiler_params=params(16),
+    )(x, parts, cot, w_self, w_neigh, bias)
+
+
+def gathered_kernel(received):
+    n, rows, lanes = received.shape
+    tiles = rows - 2 * PART
+
+    def body(ref, out):
+        total = None
+        for d in range(n):
+            out[d * tiles : (d + 1) * tiles, :] = ref[d, 0:tiles, :]
+            part = ref[d, tiles:rows, :].astype(F32)
+            total = part if total is None else total + part
+        out[n * tiles :, :] = total.astype(BF16)
+
+    return pl.pallas_call(
+        body,
+        out_shape=jax.ShapeDtypeStruct((n * tiles + 2 * PART, lanes), BF16),
+        in_specs=[VMEM],
+        out_specs=VMEM,
+        compiler_params=params(16),
+    )(received)
+
+
+def rider_kernel(mine, theirs):
+    at = mine.shape[0] - 2 * PART
+
+    def body(a_ref, b_ref, out):
+        total = (a_ref[at:, :].astype(F32) + b_ref[at:, :].astype(F32)).astype(BF16)
+        for t in range(2):
+            out[0:64, t * TILE : (t + 1) * TILE] = total[t * 64 : (t + 1) * 64]
+            out[64:PART, t * TILE : (t + 1) * TILE] = total[128 + t * 16 : 128 + (t + 1) * 16]
+
+    return pl.pallas_call(
+        body,
+        out_shape=jax.ShapeDtypeStruct((PART, 2 * TILE), BF16),
+        in_specs=[VMEM] * 2,
+        out_specs=VMEM,
+        compiler_params=params(16),
+    )(mine, theirs)
 
 
 def hop_kernel(terms, moving, w):
     refs = [t[0] if isinstance(t, tuple) else t for t in terms]
     at = [t[1] if isinstance(t, tuple) else None for t in terms]
-    rows, width = refs[0].shape[-2:]
+    width = refs[0].shape[-1]
+    rows = width
+    ins = refs + [v for v in (moving, w) if v is not None and v is not False]
 
     def body(*refs):
-        out, rider = refs[-1], refs[-2]
+        out = refs[-1]
         total = None
         for ref, i in zip(refs, at):
-            term = (ref[...] if i is None else ref[i]).astype(F32)
+            term = (ref[0:rows, :] if i is None else ref[i]).astype(F32)
             total = term if total is None else total + term
-        if moving is None:
-            out[rows:, :] = rider[...]
-        else:
-            total = total + rider[0:rows, :].astype(F32)
-            out[rows:, :] = rider[rows:, :]
+        if moving is not None:
+            total = total + refs[len(at)][0:rows, :].astype(F32)
         out[0:rows, :] = total.astype(BF16)
-
-    ins = refs + [w if moving is None else moving]
-    return pl.pallas_call(
-        body,
-        out_shape=jax.ShapeDtypeStruct((rows + PART, width), BF16),
+        if w is None:
+            out[rows:, :] = refs[len(at)][rows:, :]
+        elif w is not False:
+            out[rows:, :] = refs[-2][...]
+
+    return pl.pallas_call(
+        body,
+        out_shape=jax.ShapeDtypeStruct((rows + (0 if w is False else PART), width), BF16),
         in_specs=[VMEM] * len(ins),
         out_specs=VMEM,
         compiler_params=params(16),
@@ -323,13 +358,13 @@
     def body(*refs):
         out, all_ref = refs[-2:]
         z = axes()[0]
-        all_ref[z] = refs[0][...]
+        all_ref[z & 3] = refs[0][...]
         for j in range(len(ups)):
-            all_ref[(z - 1 - j) & (NZ - 1)] = refs[1 + j][rows:, :]
+            all_ref[(z - 1 - j) & 3] = refs[1 + j][rows:, :]
         for j in range(len(downs)):
-            all_ref[(z + 1 + j) & (NZ - 1)] = refs[1 + len(ups) + j][rows:, :]
+            all_ref[(z + 1 + j) & 3] = refs[1 + len(ups) + j][rows:, :]
         total = all_ref[0].astype(F32)
-        for i in range(1, NZ):
+        for i in range(1, n):
             total = total + all_ref[i].astype(F32)
         out[...] = total.astype(BF16)
 
@@ -338,38 +373,55 @@
         out_shape=jax.ShapeDtypeStruct(w.shape, BF16),
         in_specs=[VMEM] * n,
         out_specs=VMEM,
-        scratch_shapes=[pltpu.VMEM((NZ,) + w.shape, BF16)],
+        scratch_shapes=[pltpu.VMEM((n,) + w.shape, BF16)],
         compiler_params=params(16),
     )(w, *ups, *downs)
 
 
-def final_body(own_ref, t_ref, up_ref, down_ref, y_ref, w0_ref, w1_ref, gf_ref, gs_ref, gn_ref, gb_ref):
-    core = axes()[4]
-    f = t_ref.shape[0]
-    spread = (
-        t_ref[...].astype(F32) + up_ref[0:f, :].astype(F32) + down_ref[0:f, :].astype(F32) + y_ref[...].astype(F32)
-    )
-    gf_ref[...] = (own_ref[...] + spread.T).astype(BF16)
-
-    def write(first, second):
-        gs_ref[...] = first[0:f, :].astype(F32)
-        gn_ref[...] = second[0:f, :].astype(F32)
-        gb_ref[...] = first[f:PART, :].astype(F32)[0:1]
-
-    pl.when(core == 0)(lambda: write(w0_ref, w1_ref))
-    pl.when(core == 1)(lambda: write(w1_ref, w0_ref))
-
-
-def final_kernel(own, t, up, down, y, w0, w1):
+def features_kernel(own, t, up, down, y):
     n, f = own.shape
+
+    def body(own_ref, t_ref, up_ref, down_ref, y_ref, out):
+        spread = (
+            t_ref[...].astype(F32) + up_ref[0:f, :].astype(F32) + down_ref[0:f, :].astype(F32) + y_ref[...].astype(F32)
+        )
+        out[...] = (own_ref[...] + spread.T).astype(BF16)
+
+    return pl.pallas_call(
+        body,
+        out_shape=jax.ShapeDtypeStruct((n, f), BF16),
+        in_specs=[VMEM] * 5,
+        out_specs=VMEM,
+        compiler_params=params(16),
+    )(own, t, up, down, y)
+
+
+def weights_kernel(pairs):
+    f = pairs[0].shape[1]
+
+    def body(*refs):
+        gs_ref, gn_ref, gb_ref = refs[-3:]
+        z, yl, yh, x, core = axes()
+        for j in range(NX):
+            at = (x + j) & (NX - 1)
+            rows = pl.ds(pl.multiple_of(at * 64, 64), 64)
+            for h, out in enumerate((gs_ref, gn_ref)):
+                start = pl.multiple_of((yh ^ h) * PART, 16)
+                out[rows, :] = refs[j][pl.ds(start, 64), :].astype(F32)
+
+            @pl.when(at == 0)
+            def _():
+                start = pl.multiple_of(yh * PART + 64, 16)
+                gb_ref[...] = refs[j][pl.ds(start, 16), :].astype(F32)[0:1]
+
     sq = jax.ShapeDtypeStruct((f, f), F32)
     return pl.pallas_call(
-        final_body,
-        out_shape=[jax.ShapeDtypeStruct((n, f), BF16), sq, sq, jax.ShapeDtypeStruct((1, f), F32)],
-        in_specs=[VMEM] * 7,
-        out_specs=[VMEM] * 4,
-        compiler_params=params(16),
-    )(own, t, up, down, y, w0, w1)
+        body,
+        out_shape=[sq, sq, jax.ShapeDtypeStruct((1, f), F32)],
+        in_specs=[VMEM] * NX,
+        out_specs=[VMEM] * 3,
+        compiler_params=params(16),
+    )(*pairs)
 
 
 def add(*terms):
@@ -379,73 +431,55 @@
     return total.astype(BF16)
 
 
-def flip_z(value, bit):
-    return permute(value, dz=lambda z: (z ^ bit) - z)
-
-
 def after(value, *done):
     return lax.optimization_barrier((value, *done))[0]
 
 
 def local(features, w_self, w_neigh, bias, cotangent, tile_values, tile_rows, tile_cols, tile_counts):
     width = features.shape[1]
-    lists, lens = list_kernel(tile_rows[0, 0], tile_cols[0, 0], tile_counts[0, 0])
+    lists, lens = list_kernel(tile_rows[0, 0].T, tile_cols[0, 0].T, tile_counts[0, 0])
     tiles = load_kernel(tile_values.reshape((-1,) + tile_values.shape[4:]))
 
     together = lax.optimization_barrier
-    up, down = permute(features, dz=1), permute(features, dz=-1)
     got = {(0, 0): features}
-    up, down, got[0, 1], lists = together((up, down, permute(features, dyl=1), lists))
-    acc = None
-    for k in (1, 2, 3, 4):
-        got[-k, 0], got[k, 0] = up, down
-        here = (up, down)
-        if k < 3:
-            up, down = permute(up, dz=1), permute(down, dz=-1)
-        elif k == 3:
-            up = down = permute(up, dz=1)
-        there = permute(join_kernel(here) if k < 4 else up, dyl=1)
+    got[0, 1] = after(permute(features, dyl=1), tiles)
+    for k in (1, 2, 3):
+        for dy in (0, 1):
+            got[-k, dy] = permute(got[1 - k, dy], dz=1)
+            got[k, dy] = permute(got[k - 1, dy], dz=-1)
         if k == 1:
-            up, down, there, tiles = together((up, down, there, tiles))
-        else:
-            acc = forward_kernel((k - 2,), lists, lens, tiles, got, acc, False)
-            up, down, there, acc = together((up, down, there, acc))
-        rows = features.shape[0]
-        got[-k, 1], got[k, 1] = (there[:rows], there[rows:]) if k < 4 else (there, there)
+            got[1, 0] = after(got[1, 0], lists)
+        if k == 2:
+            acc = forward_kernel((0,), lists, lens, tiles, got, None, False)
+            got[2, 1], acc = together((got[2, 1], acc))
+        if k == 3:
+            acc = forward_kernel((1,), lists, lens, tiles, got, acc, False)
+            got[3, 1], acc = together((got[3, 1], acc))
+    got[4, 0] = permute(got[-3, 0], dz=1)
+    got[4, 1] = permute(got[3, 1], dz=-1)
+    acc = forward_kernel((2,), lists, lens, tiles, got, acc, False)
     partial = forward_kernel((3,), lists, lens, tiles, got, acc, True)
 
+    chips = [[q * NC + c for q in range(NYH * NX)] for c in range(NC)]
     partial = partial.reshape(2, 16 * TILE, width)
-    half = add(partial[0], permute(partial[1], dc=1)).reshape(4, 4 * TILE, width)
-    quarter = add(
-        half[0], permute(half[1], dx=1), permute(half[3], dx=-1), permute(half[2], dx=2)
-    ).reshape(2, 2 * TILE, width)
-    other = permute(quarter[1], dyh=1)
-
-    output, dz, agg, dagg = dense_kernel(
-        features, quarter[0], other, cotangent, w_self, w_neigh, bias.reshape(1, width)
-    )
-
-    parts, own = weight_kernel(features, agg, dz, w_self)
-    w = add(parts[0], permute(parts[1], dc=1))
-    dagg_y, w = together((permute(dagg, dyh=1), w))
-    pair = join_kernel([dagg, dagg_y])
-    w = add(w, permute(w, dyl=1))
-    from_left, from_right, w = together((permute(pair, dx=1), permute(pair, dx=-1), w))
-    w = add(w, permute(w, dyh=1))
-    left, right, w = together((permute(from_left[0:2], dx=1), permute(from_right[2:4], dx=-1), w))
-    mine = join_kernel([pair, from_right, left, right, from_left])
-    w = add(w, permute(w, dx=lambda x: (x ^ 1) - x))
-    theirs, w = together((permute(mine, dc=1), w))
+    half = add(partial[0], permute(partial[1], dc=1)).reshape(8, 2 * TILE, width)
+    parts = lax.all_to_all(half, "rep", 0, 0, axis_index_groups=chips, tiled=True)
+
+    output, own, send = dense_kernel(features, parts, cotangent, w_self, w_neigh, bias.reshape(1, width))
+
+    mine = gathered_kernel(lax.all_to_all(send, "rep", 0, 0, axis_index_groups=chips, tiled=True))
+    theirs = permute(mine, dc=1)
 
     def products(k):
         return backward_kernel(k, lists, lens, tiles, mine, theirs)
 
+    w = rider_kernel(mine, theirs)
     (t4,), u4 = products(3)
-    w, theirs, u4 = together((w, theirs, u4))
+    theirs, u4 = together((theirs, u4))
     (t3, t3d), u3 = products(2)
-    y4, w, theirs, u3 = together(
-        (permute(u4, dyl=1), add(w, permute(w, dx=lambda x: 3 - 2 * x)), theirs, u3)
-    )
+    y4 = permute(u4, dyl=1)
+    w = add(w, permute(w, dz=4))
+    y4, w, theirs, u3 = together((y4, w, theirs, u3))
     (t2, t2d), u2 = products(1)
     up1, y3, theirs, u2 = together(
         (permute(hop_kernel([t4, (y4, 0)], None, w), dz=1), permute(u3, dyl=1), theirs, u2)
@@ -453,29 +487,34 @@
     (t0, t1, t1d), u1 = products(0)
     up2, down1, y2, u1 = together(
         (
-            permute(hop_kernel([t3, (y3, 0)], up1, w), dz=1),
+            permute(hop_kernel([t3, (y3, 0)], up1, None), dz=1),
             permute(hop_kernel([t3d, (y3, 1)], None, w), dz=-1),
             permute(u2, dyl=1),
             u1,
         )
     )
+    w = total_kernel(w, [up1, up2], [down1])
+    u1 = u1.reshape(3 * width, -1)
     up3, down2, y1 = together(
         (
-            permute(hop_kernel([t2, (y2, 0)], up2, w), dz=1),
-            permute(hop_kernel([t2d, (y2, 1)], down1, w), dz=-1),
-            permute(u1[1:], dyl=1),
+            permute(hop_kernel([t2, (y2, 0)], up2, False), dz=1),
+            permute(hop_kernel([t2d, (y2, 1)], down1, False), dz=-1),
+            permute(join_kernel([u1[width:], w]), dyl=1),
         )
     )
-    up4, down3, y0 = together(
+    w = add(w, y1[2 * width :])
+    up4, down3, y0, w_y = together(
         (
-            permute(hop_kernel([t1, (y1, 0)], up3, w), dz=1),
-            permute(hop_kernel([t1d, (y1, 1)], down2, w), dz=-1),
-            permute(u1[0], dyl=1),
+            permute(hop_kernel([t1, y1], up3, False), dz=1),
+            permute(hop_kernel([t1d, (y1, slice(width, 2 * width))], down2, False), dz=-1),
+            permute(u1[:width], dyl=1),
+            permute(w, dyh=1),
         )
     )
-    w = total_kernel(w, [up1, up2, up3, up4], [down1, down2, down3])
-    grad_features, grad_self, grad_neigh, grad_bias = final_kernel(
-        own, t0, up4, down3, y0, w, permute(w, dc=1)
+    grad_features = features_kernel(own, t0, up4, down3, y0)
+    pair = join_kernel([w, w_y])
+    grad_self, grad_neigh, grad_bias = weights_kernel(
+        [pair, permute(pair, dx=-1), permute(pair, dx=2), permute(pair, dx=1)]
     )
     return (output, grad_features, grad_self, grad_neigh, grad_bias.reshape(width))
 

time: 162 us -> 150 us (0.926); the launches traced: 159 us -> 150 us
  blocking collectives: 0 us -> 45.7 us
  waiting for transfers between devices: 70.7 us -> 35.1 us
  starting transfers between devices: 59.6 us -> 47.8 us
  Pallas kernels: 21.3 us -> 16.7 us
  local copies, waits for them, and re-layouts: 5.33 us -> 3.01 us
    all_to_all x0 -> x2, blocking collectives: none -> 45.7 us  [the longest x1 23.1 us: local(): lax.all_to_all(half, 'rep', 0, 0, axis_index_groups=chips, tiled=True)]
    ppermute x41 -> x34, waiting for transfers between devices: 70.7 us -> 35.1 us  [permute(): return lax.ppermute(value, ('blk', 'rep'), pairs)]
    ppermute x41 -> x34, starting transfers between devices: 59.6 us -> 47.8 us  [permute(): return lax.ppermute(value, ('blk', 'rep'), pairs)]
    unnamed x16 -> x18, local copies, waits for them, and re-layouts: 5 us -> 2.81 us
    pallas_call x4, Pallas kernels: 7.58 us -> 5.75 us  [forward_kernel(): pl.pallas_call(body, out_shape=out_shape, in_specs=[SMEM] * 2 + [VMEM] *...]
    pallas_call x4, Pallas kernels: 7.05 us -> 5.25 us  [backward_kernel(): pl.pallas_call(body, out_shape=[jax.ShapeDtypeStruct((width, 2 * TILE), B...]
  transfers between devices with their start and end apart: 41 -> 34, of which waited for: 24 -> 14; matrix products, arithmetic and copies ran while one was open for 1% -> 0% of each run, Pallas kernels for 10% -> 9%
where the time goes in v2:
time: 150 us
  starting transfers between devices  47.8 us (32%)
  blocking collectives  45.7 us (30%)
  waiting for transfers between devices  35.1 us (23%)
  Pallas kernels  16.7 us (11%)
  local copies, waits for them, and re-layouts  3.01 us (2%)
    ppermute x34, starting transfers between devices, permute(): return lax.ppermute(value, ('blk', 'rep'), pairs)  47.8 us
    ppermute x34, waiting for transfers between devices, permute(): return lax.ppermute(value, ('blk', 'rep'), pairs)  35.1 us
    all_to_all x1, blocking collectives, local(): lax.all_to_all(half, 'rep', 0, 0, axis_index_groups=chips, tiled=True)  23.1 us
    all_to_all x1, blocking collectives, local(): lax.all_to_all(send, 'rep', 0, 0, axis_index_groups=chips, tiled=True)  22.6 us
    pallas_call x4, Pallas kernels, forward_kernel(): pl.pallas_call(body, out_shape=out_shape, in_specs=[SMEM] * 2 + [VMEM] *...  5.75 us
    pallas_call x4, Pallas kernels, backward_kernel(): pl.pallas_call(body, out_shape=[jax.ShapeDtypeStruct((width, 2 * TILE), B...  5.25 us
  transfers between devices with their start and end apart: 34, of which 14 were waited for; matrix products, arithmetic and copies ran while one was open for 0% of the time, Pallas kernels for 9%

profile of v2, /device:TPU:8, one launch (start us, length us, event | category | flops | bytes accessed | tf_op | source)
XLA Modules:
  0.0 149.7 jit_solution(1643806143584379173)
XLA Ops:
  0.6 2.3 %collective-permute-start.4 = (bf16[256,256]{1,0:T(8,128)(2,1)}, bf16[256,256]{1,0:T(8,128)(2,1)S(1)}, u32[]{:S(2)}, u32[]{:S(2)}) collective-permute-start(bf16[256,256]{1,0:T(8,128)(2,1)} %x_ref.1), channel_id=1, source_target_pairs={{0,16},{1,17},{2,18},{3,19},{4,20},{5,21},{6,22},{7,23},{8,24},{9,... | collective-permute-start | bytes 393224 | tf_op jit(solution)/shard_map/ppermute | solution.py:29
  3.1 2.8 %copy-done = bf16[1,1,16,12,128,128]{5,4,3,2,1,0:T(8,128)(2,1)S(1)} copy-done((bf16[1,1,16,12,128,128]{5,4,3,2,1,0:T(8,128)(2,1)S(1)}, bf16[1,1,16,12,128,128]{5,4,3,2,1,0:T(8,128)(2,1)}, u32[]{:S(2)}) %copy-start) | copy-done | bytes 6291480
  6.3 5.7 %collective-permute-start.5 = (bf16[256,256]{1,0:T(8,128)(2,1)S(1)}, bf16[256,256]{1,0:T(8,128)(2,1)S(1)}, u32[]{:S(2)}, u32[]{:S(2)}) collective-permute-start(bf16[256,256]{1,0:T(8,128)(2,1)S(1)} %collective-permute-done.4.refs_1_), channel_id=1, source_target_pairs={{0,224},{1,225},{2,226},{3,227},{4,228},{5,229},{6,230},{7,231},{8... | collective-permute-start | bytes 393224 | tf_op jit(solution)/shard_map/ppermute | solution.py:29
  15.3 3.7 %collective-permute-start.6 = (bf16[256,256]{1,0:T(8,128)(2,1)S(1)}, bf16[256,256]{1,0:T(8,128)(2,1)S(1)}, u32[]{:S(2)}, u32[]{:S(2)}) collective-permute-start(bf16[256,256]{1,0:T(8,128)(2,1)S(1)} %collective-permute-done.5.refs_3_), channel_id=1, source_target_pairs={{0,224},{1,225},{2,226},{3,227},{4,228},{5,229},{6,230},{7,231},{8... | collective-permute-start | bytes 393224 | tf_op jit(solution)/shard_map/ppermute | solution.py:29
  19.0 2.1 %shard_map.128 = (s32[4,88]{1,0:T(4,128)S(1)}, s32[4]{0:T(128)S(1)}) custom-call(s32[12,16]{1,0:T(8,128)S(1)} %get-tuple-element.102.rows_ref, s32[12,16]{1,0:T(8,128)S(1)} %get-tuple-element.101.cols_ref, s32[16]{0:T(128)S(1)} %bitcast.23), custom_call_target="tpu_custom_call" | custom-call | tf_op jit(solution)/shard_map/pallas_call | solution.py:76
  24.7 4.1 %collective-permute-start.9 = (bf16[256,256]{1,0:T(8,128)(2,1)S(1)}, bf16[256,256]{1,0:T(8,128)(2,1)S(1)}, u32[]{:S(2)}, u32[]{:S(2)}) collective-permute-start(bf16[256,256]{1,0:T(8,128)(2,1)S(1)} %collective-permute-done.6.refs_1_), channel_id=1, source_target_pairs={{0,224},{1,225},{2,226},{3,227},{4,228},{5,229},{6,230},{7,231},{8... | collective-permute-start | bytes 393224 | tf_op jit(solution)/shard_map/ppermute | solution.py:29
  29.2 1.7 %collective-permute-start.14 = (bf16[256,256]{1,0:T(8,128)(2,1)S(1)}, bf16[256,256]{1,0:T(8,128)(2,1)S(1)}, u32[]{:S(2)}, u32[]{:S(2)}) collective-permute-start(bf16[256,256]{1,0:T(8,128)(2,1)S(1)} %collective-permute-done.11.refs_3_), channel_id=1, source_target_pairs={{0,32},{1,33},{2,34},{3,35},{4,36},{5,37},{6,38},{7,39},{8,40},{9,... | collective-permute-start | bytes 393224 | tf_op jit(solution)/shard_map/ppermute | solution.py:29
  32.5 3.7 %collective-permute-start.12 = (bf16[256,256]{1,0:T(8,128)(2,1)S(1)}, bf16[256,256]{1,0:T(8,128)(2,1)S(1)}, u32[]{:S(2)}, u32[]{:S(2)}) collective-permute-start(bf16[256,256]{1,0:T(8,128)(2,1)S(1)} %collective-permute-done.9.refs_1_), channel_id=1, source_target_pairs={{0,224},{1,225},{2,226},{3,227},{4,228},{5,229},{6,230},{7,231},{8... | collective-permute-start | bytes 393224 | tf_op jit(solution)/shard_map/ppermute | solution.py:29
  40.5 2.6 %collective-permute-done.15 = bf16[2048,256]{1,0:T(8,128)(2,1)S(1)} collective-permute-done((bf16[2048,256]{1,0:T(8,128)(2,1)S(1)}, bf16[2048,256]{1,0:T(8,128)(2,1)S(1)}, u32[]{:S(2)}, u32[]{:S(2)}) %collective-permute-start.15) | collective-permute-done | bytes 1048608 | tf_op jit(solution)/shard_map/ppermute | solution.py:29
  43.6 23.1 %all_to_all.10.parts_ref = bf16[8,256,256]{2,1,0:T(8,128)(2,1)S(1)} all-to-all(bf16[8,256,256]{2,1,0:T(8,128)(2,1)S(1)} %bitcast.24), channel_id=1, replica_groups={{0,2,4,6,8,10,12,14},{1,3,5,7,9,11,13,15},{16,18,20,22,24,26,28,30},{17..., dimensions={0} | all-to-all | bytes 2097152 | tf_op jit(solution)/shard_map/all_to_all | solution.py:466
  67.7 22.6 %all_to_all.11.ref = bf16[8,672,128]{2,1,0:T(8,128)(2,1)S(1)} all-to-all(bf16[8,672,128]{2,1,0:T(8,128)(2,1)S(1)} %get-tuple-element.62), channel_id=1, replica_groups={{0,2,4,6,8,10,12,14},{1,3,5,7,9,11,13,15},{16,18,20,22,24,26,28,30},{17..., dimensions={0} | all-to-all | bytes 2752512 | tf_op jit(solution)/shard_map/all_to_all | solution.py:470
  90.5 2.7 %collective-permute-done.16.their_ref.b_ref = bf16[4256,128]{1,0:T(8,128)(2,1)S(1)} collective-permute-done((bf16[4256,128]{1,0:T(8,128)(2,1)S(1)}, bf16[4256,128]{1,0:T(8,128)(2,1)S(1)}, u32[]{:S(2)}, u32[]{:S(2)}) %collective-permute-start.16) | collective-permute-done | bytes 1089568 | tf_op jit(solution)/shard_map/ppermute | solution.py:29
  93.2 4.4 %collective-permute-start.18 = (bf16[80,256]{1,0:T(8,128)(2,1)S(1)}, bf16[80,256]{1,0:T(8,128)(2,1)S(1)}, u32[]{:S(2)}, u32[]{:S(2)}) collective-permute-start(bf16[80,256]{1,0:T(8,128)(2,1)S(1)} %shard_map.137), channel_id=1, source_target_pairs={{0,128},{1,129},{2,130},{3,131},{4,132},{5,133},{6,134},{7,135},{8... | collective-permute-start | bytes 122888 | tf_op jit(solution)/shard_map/ppermute | solution.py:29
  101.7 2.6 %collective-permute-done.17.refs_1_ = bf16[1,256,256]{2,1,0:T(8,128)(2,1)S(1)} collective-permute-done((bf16[1,256,256]{2,1,0:T(8,128)(2,1)S(1)}, bf16[1,256,256]{2,1,0:T(8,128)(2,1)S(1)}, u32[]{:S(2)}, u32[]{:S(2)}) %collective-permute-start.17) | collective-permute-done | bytes 131104 | tf_op jit(solution)/shard_map/ppermute | solution.py:29
  104.3 1.7 %collective-permute-start.20 = (bf16[2,256,256]{2,1,0:T(8,128)(2,1)S(1)}, bf16[2,256,256]{2,1,0:T(8,128)(2,1)S(1)}, u32[]{:S(2)}, u32[]{:S(2)}) collective-permute-start(bf16[2,256,256]{2,1,0:T(8,128)(2,1)S(1)} %get-tuple-element.70), channel_id=1, source_target_pairs={{0,16},{1,17},{2,18},{3,19},{4,20},{5,21},{6,22},{7,23},{8,24},{9,... | collective-permute-start | bytes 786440 | tf_op jit(solution)/shard_map/ppermute | solution.py:29
  107.5 5.4 %collective-permute-done.19.refs_2_.refs_1_ = bf16[336,256]{1,0:T(8,128)(2,1)S(1)} collective-permute-done((bf16[336,256]{1,0:T(8,128)(2,1)S(1)}, bf16[336,256]{1,0:T(8,128)(2,1)S(1)}, u32[]{:S(2)}, u32[]{:S(2)}) %collective-permute-start.19) | collective-permute-done | bytes 172064 | tf_op jit(solution)/shard_map/ppermute | solution.py:29
  114.0 2.6 %collective-permute-start.22 = (bf16[336,256]{1,0:T(8,128)(2,1)S(1)}, bf16[336,256]{1,0:T(8,128)(2,1)S(1)}, u32[]{:S(2)}, u32[]{:S(2)}) collective-permute-start(bf16[336,256]{1,0:T(8,128)(2,1)S(1)} %shard_map.143), channel_id=1, source_target_pairs={{0,224},{1,225},{2,226},{3,227},{4,228},{5,229},{6,230},{7,231},{8... | collective-permute-start | bytes 516104 | tf_op jit(solution)/shard_map/ppermute | solution.py:29
  119.5 4.0 %collective-permute-done.21.refs_2_ = bf16[336,256]{1,0:T(8,128)(2,1)S(1)} collective-permute-done((bf16[336,256]{1,0:T(8,128)(2,1)S(1)}, bf16[336,256]{1,0:T(8,128)(2,1)S(1)}, u32[]{:S(2)}, u32[]{:S(2)}) %collective-permute-start.21) | collective-permute-done | bytes 172064 | tf_op jit(solution)/shard_map/ppermute | solution.py:29
  125.1 2.1 %collective-permute-start.24 = (bf16[256,256]{1,0:T(8,128)(2,1)S(1)}, bf16[256,256]{1,0:T(8,128)(2,1)S(1)}, u32[]{:S(2)}, u32[]{:S(2)}) collective-permute-start(bf16[256,256]{1,0:T(8,128)(2,1)S(1)} %shard_map.144), channel_id=1, source_target_pairs={{0,32},{1,33},{2,34},{3,35},{4,36},{5,37},{6,38},{7,39},{8,40},{9,... | collective-permute-start | bytes 393224 | tf_op jit(solution)/shard_map/ppermute | solution.py:29
  128.1 3.0 %collective-permute-done.25.refs_2_ = bf16[256,256]{1,0:T(8,128)(2,1)S(1)} collective-permute-done((bf16[256,256]{1,0:T(8,128)(2,1)S(1)}, bf16[256,256]{1,0:T(8,128)(2,1)S(1)}, u32[]{:S(2)}, u32[]{:S(2)}) %collective-permute-start.25) | collective-permute-done | bytes 131104 | tf_op jit(solution)/shard_map/ppermute | solution.py:29
  132.6 2.1 %collective-permute-start.27 = (bf16[256,256]{1,0:T(8,128)(2,1)S(1)}, bf16[256,256]{1,0:T(8,128)(2,1)S(1)}, u32[]{:S(2)}, u32[]{:S(2)}) collective-permute-start(bf16[256,256]{1,0:T(8,128)(2,1)S(1)} %shard_map.148), channel_id=1, source_target_pairs={{0,32},{1,33},{2,34},{3,35},{4,36},{5,37},{6,38},{7,39},{8,40},{9,... | collective-permute-start | bytes 393224 | tf_op jit(solution)/shard_map/ppermute | solution.py:29
  135.4 4.9 %collective-permute-done.30.refs_1_ = bf16[80,256]{1,0:T(8,128)(2,1)S(1)} collective-permute-done((bf16[80,256]{1,0:T(8,128)(2,1)S(1)}, bf16[80,256]{1,0:T(8,128)(2,1)S(1)}, u32[]{:S(2)}, u32[]{:S(2)}) %collective-permute-start.30) | collective-permute-done | bytes 40992 | tf_op jit(solution)/shard_map/ppermute | solution.py:29
  141.7 1.6 %collective-permute-start.32 = (bf16[160,256]{1,0:T(8,128)(2,1)S(1)}, bf16[160,256]{1,0:T(8,128)(2,1)S(1)}, u32[]{:S(2)}, u32[]{:S(2)}) collective-permute-start(bf16[160,256]{1,0:T(8,128)(2,1)S(1)} %shard_map.151.refs_0_), channel_id=1, source_target_pairs={{0,4},{1,5},{2,6},{3,7},{4,0},{5,1},{6,2},{7,3},{8,12},{9,13},{10,... | collective-permute-start | bytes 245768 | tf_op jit(solution)/shard_map/ppermute | solution.py:29
  144.9 2.8 %collective-permute-done.32.refs_2_ = bf16[160,256]{1,0:T(8,128)(2,1)S(1)} collective-permute-done((bf16[160,256]{1,0:T(8,128)(2,1)S(1)}, bf16[160,256]{1,0:T(8,128)(2,1)S(1)}, u32[]{:S(2)}, u32[]{:S(2)}) %collective-permute-start.32) | collective-permute-done | bytes 81952 | tf_op jit(solution)/shard_map/ppermute | solution.py:29
  (96 shorter events, 34.5 us)
Async XLA Ops:
  2.9 11.2 %collective-permute-start = (bf16[256,256]{1,0:T(8,128)(2,1)}, bf16[256,256]{1,0:T(8,128)(2,1)S(1)}, u32[]{:S(2)}, u32[]{:S(2)}) collective-permute-start(bf16[256,256]{1,0:T(8,128)(2,1)} %x_ref.1), channel_id=1, source_target_pairs={{0,32},{1,33},{2,34},{3,35},{4,36},{5,37},{6,38},{7,39},{8,40},{9,... | collective-permute-start | bytes 393224 | tf_op jit(solution)/shard_map/ppermute | solution.py:29
  6.3 9.0 %collective-permute-start.5 = (bf16[256,256]{1,0:T(8,128)(2,1)S(1)}, bf16[256,256]{1,0:T(8,128)(2,1)S(1)}, u32[]{:S(2)}, u32[]{:S(2)}) collective-permute-start(bf16[256,256]{1,0:T(8,128)(2,1)S(1)} %collective-permute-done.4.refs_1_), channel_id=1, source_target_pairs={{0,224},{1,225},{2,226},{3,227},{4,228},{5,229},{6,230},{7,231},{8... | collective-permute-start | bytes 393224 | tf_op jit(solution)/shard_map/ppermute | solution.py:29
  12.0 9.1 %collective-permute-start.7 = (bf16[256,256]{1,0:T(8,128)(2,1)S(1)}, bf16[256,256]{1,0:T(8,128)(2,1)S(1)}, u32[]{:S(2)}, u32[]{:S(2)}) collective-permute-start(bf16[256,256]{1,0:T(8,128)(2,1)S(1)} %copy-done.1), channel_id=1, source_target_pairs={{0,224},{1,225},{2,226},{3,227},{4,228},{5,229},{6,230},{7,231},{8... | collective-permute-start | bytes 393224 | tf_op jit(solution)/shard_map/ppermute | solution.py:29
  13.0 9.0 %collective-permute-start.8 = (bf16[256,256]{1,0:T(8,128)(2,1)S(1)}, bf16[256,256]{1,0:T(8,128)(2,1)S(1)}, u32[]{:S(2)}, u32[]{:S(2)}) collective-permute-start(bf16[256,256]{1,0:T(8,128)(2,1)S(1)} %collective-permute-done.4.refs_1_), channel_id=1, source_target_pairs={{0,32},{1,33},{2,34},{3,35},{4,36},{5,37},{6,38},{7,39},{8,40},{9,... | collective-permute-start | bytes 393224 | tf_op jit(solution)/shard_map/ppermute | solution.py:29
  14.1 9.2 %collective-permute-start.1 = (bf16[256,256]{1,0:T(8,128)(2,1)S(1)}, bf16[256,256]{1,0:T(8,128)(2,1)S(1)}, u32[]{:S(2)}, u32[]{:S(2)}) collective-permute-start(bf16[256,256]{1,0:T(8,128)(2,1)S(1)} %collective-permute-done.refs_4_), channel_id=1, source_target_pairs={{0,32},{1,33},{2,34},{3,35},{4,36},{5,37},{6,38},{7,39},{8,40},{9,... | collective-permute-start | bytes 393224 | tf_op jit(solution)/shard_map/ppermute | solution.py:29
  15.3 9.4 %collective-permute-start.6 = (bf16[256,256]{1,0:T(8,128)(2,1)S(1)}, bf16[256,256]{1,0:T(8,128)(2,1)S(1)}, u32[]{:S(2)}, u32[]{:S(2)}) collective-permute-start(bf16[256,256]{1,0:T(8,128)(2,1)S(1)} %collective-permute-done.5.refs_3_), channel_id=1, source_target_pairs={{0,224},{1,225},{2,226},{3,227},{4,228},{5,229},{6,230},{7,231},{8... | collective-permute-start | bytes 393224 | tf_op jit(solution)/shard_map/ppermute | solution.py:29
  21.1 7.7 %collective-permute-start.10 = (bf16[256,256]{1,0:T(8,128)(2,1)S(1)}, bf16[256,256]{1,0:T(8,128)(2,1)S(1)}, u32[]{:S(2)}, u32[]{:S(2)}) collective-permute-start(bf16[256,256]{1,0:T(8,128)(2,1)S(1)} %collective-permute-done.7.refs_2_), channel_id=1, source_target_pairs={{0,224},{1,225},{2,226},{3,227},{4,228},{5,229},{6,230},{7,231},{8... | collective-permute-start | bytes 393224 | tf_op jit(solution)/shard_map/ppermute | solution.py:29
  22.0 7.2 %collective-permute-start.11 = (bf16[256,256]{1,0:T(8,128)(2,1)S(1)}, bf16[256,256]{1,0:T(8,128)(2,1)S(1)}, u32[]{:S(2)}, u32[]{:S(2)}) collective-permute-start(bf16[256,256]{1,0:T(8,128)(2,1)S(1)} %collective-permute-done.8.refs_5_), channel_id=1, source_target_pairs={{0,32},{1,33},{2,34},{3,35},{4,36},{5,37},{6,38},{7,39},{8,40},{9,... | collective-permute-start | bytes 393224 | tf_op jit(solution)/shard_map/ppermute | solution.py:29
  23.2 7.6 %collective-permute-start.2 = (bf16[256,256]{1,0:T(8,128)(2,1)S(1)}, bf16[256,256]{1,0:T(8,128)(2,1)S(1)}, u32[]{:S(2)}, u32[]{:S(2)}) collective-permute-start(bf16[256,256]{1,0:T(8,128)(2,1)S(1)} %collective-permute-done.1.refs_2_), channel_id=1, source_target_pairs={{0,32},{1,33},{2,34},{3,35},{4,36},{5,37},{6,38},{7,39},{8,40},{9,... | collective-permute-start | bytes 393224 | tf_op jit(solution)/shard_map/ppermute | solution.py:29
  24.7 7.8 %collective-permute-start.9 = (bf16[256,256]{1,0:T(8,128)(2,1)S(1)}, bf16[256,256]{1,0:T(8,128)(2,1)S(1)}, u32[]{:S(2)}, u32[]{:S(2)}) collective-permute-start(bf16[256,256]{1,0:T(8,128)(2,1)S(1)} %collective-permute-done.6.refs_1_), channel_id=1, source_target_pairs={{0,224},{1,225},{2,226},{3,227},{4,228},{5,229},{6,230},{7,231},{8... | collective-permute-start | bytes 393224 | tf_op jit(solution)/shard_map/ppermute | solution.py:29
  28.8 7.3 %collective-permute-start.13 = (bf16[256,256]{1,0:T(8,128)(2,1)S(1)}, bf16[256,256]{1,0:T(8,128)(2,1)S(1)}, u32[]{:S(2)}, u32[]{:S(2)}) collective-permute-start(bf16[256,256]{1,0:T(8,128)(2,1)S(1)} %collective-permute-done.10.refs_0_), channel_id=1, source_target_pairs={{0,224},{1,225},{2,226},{3,227},{4,228},{5,229},{6,230},{7,231},{8... | collective-permute-start | bytes 393224 | tf_op jit(solution)/shard_map/ppermute | solution.py:29
  29.2 7.0 %collective-permute-start.14 = (bf16[256,256]{1,0:T(8,128)(2,1)S(1)}, bf16[256,256]{1,0:T(8,128)(2,1)S(1)}, u32[]{:S(2)}, u32[]{:S(2)}) collective-permute-start(bf16[256,256]{1,0:T(8,128)(2,1)S(1)} %collective-permute-done.11.refs_3_), channel_id=1, source_target_pairs={{0,32},{1,33},{2,34},{3,35},{4,36},{5,37},{6,38},{7,39},{8,40},{9,... | collective-permute-start | bytes 393224 | tf_op jit(solution)/shard_map/ppermute | solution.py:29
  30.9 6.7 %collective-permute-start.3 = (bf16[256,256]{1,0:T(8,128)(2,1)S(1)}, bf16[256,256]{1,0:T(8,128)(2,1)S(1)}, u32[]{:S(2)}, u32[]{:S(2)}) collective-permute-start(bf16[256,256]{1,0:T(8,128)(2,1)S(1)} %collective-permute-done.2.refs_2_), channel_id=1, source_target_pairs={{0,32},{1,33},{2,34},{3,35},{4,36},{5,37},{6,38},{7,39},{8,40},{9,... | collective-permute-start | bytes 393224 | tf_op jit(solution)/shard_map/ppermute | solution.py:29
  32.5 6.2 %collective-permute-start.12 = (bf16[256,256]{1,0:T(8,128)(2,1)S(1)}, bf16[256,256]{1,0:T(8,128)(2,1)S(1)}, u32[]{:S(2)}, u32[]{:S(2)}) collective-permute-start(bf16[256,256]{1,0:T(8,128)(2,1)S(1)} %collective-permute-done.9.refs_1_), channel_id=1, source_target_pairs={{0,224},{1,225},{2,226},{3,227},{4,228},{5,229},{6,230},{7,231},{8... | collective-permute-start | bytes 393224 | tf_op jit(solution)/shard_map/ppermute | solution.py:29
  93.2 8.4 %collective-permute-start.18 = (bf16[80,256]{1,0:T(8,128)(2,1)S(1)}, bf16[80,256]{1,0:T(8,128)(2,1)S(1)}, u32[]{:S(2)}, u32[]{:S(2)}) collective-permute-start(bf16[80,256]{1,0:T(8,128)(2,1)S(1)} %shard_map.137), channel_id=1, source_target_pairs={{0,128},{1,129},{2,130},{3,131},{4,132},{5,133},{6,134},{7,135},{8... | collective-permute-start | bytes 122888 | tf_op jit(solution)/shard_map/ppermute | solution.py:29
  104.3 8.6 %collective-permute-start.20 = (bf16[2,256,256]{2,1,0:T(8,128)(2,1)S(1)}, bf16[2,256,256]{2,1,0:T(8,128)(2,1)S(1)}, u32[]{:S(2)}, u32[]{:S(2)}) collective-permute-start(bf16[2,256,256]{2,1,0:T(8,128)(2,1)S(1)} %get-tuple-element.70), channel_id=1, source_target_pairs={{0,16},{1,17},{2,18},{3,19},{4,20},{5,21},{6,22},{7,23},{8,24},{9,... | collective-permute-start | bytes 786440 | tf_op jit(solution)/shard_map/ppermute | solution.py:29
  106.1 6.8 %collective-permute-start.19 = (bf16[336,256]{1,0:T(8,128)(2,1)S(1)}, bf16[336,256]{1,0:T(8,128)(2,1)S(1)}, u32[]{:S(2)}, u32[]{:S(2)}) collective-permute-start(bf16[336,256]{1,0:T(8,128)(2,1)S(1)} %shard_map.139), channel_id=1, source_target_pairs={{0,32},{1,33},{2,34},{3,35},{4,36},{5,37},{6,38},{7,39},{8,40},{9,... | collective-permute-start | bytes 516104 | tf_op jit(solution)/shard_map/ppermute | solution.py:29
  112.9 10.6 %collective-permute-start.23 = (bf16[2,256,256]{2,1,0:T(8,128)(2,1)S(1)}, bf16[2,256,256]{2,1,0:T(8,128)(2,1)S(1)}, u32[]{:S(2)}, u32[]{:S(2)}) collective-permute-start(bf16[2,256,256]{2,1,0:T(8,128)(2,1)S(1)} %get-tuple-element.81), channel_id=1, source_target_pairs={{0,16},{1,17},{2,18},{3,19},{4,20},{5,21},{6,22},{7,23},{8,24},{9,... | collective-permute-start | bytes 786440 | tf_op jit(solution)/shard_map/ppermute | solution.py:29
  116.6 6.9 %collective-permute-start.21 = (bf16[336,256]{1,0:T(8,128)(2,1)S(1)}, bf16[336,256]{1,0:T(8,128)(2,1)S(1)}, u32[]{:S(2)}, u32[]{:S(2)}) collective-permute-start(bf16[336,256]{1,0:T(8,128)(2,1)S(1)} %shard_map.142), channel_id=1, source_target_pairs={{0,32},{1,33},{2,34},{3,35},{4,36},{5,37},{6,38},{7,39},{8,40},{9,... | collective-permute-start | bytes 516104 | tf_op jit(solution)/shard_map/ppermute | solution.py:29
  123.6 8.8 %collective-permute-start.26 = (bf16[592,256]{1,0:T(8,128)(2,1)S(1)}, bf16[592,256]{1,0:T(8,128)(2,1)S(1)}, u32[]{:S(2)}, u32[]{:S(2)}) collective-permute-start(bf16[592,256]{1,0:T(8,128)(2,1)S(1)} %shard_map.147), channel_id=1, source_target_pairs={{0,16},{1,17},{2,18},{3,19},{4,20},{5,21},{6,22},{7,23},{8,24},{9,... | collective-permute-start | bytes 909320 | tf_op jit(solution)/shard_map/ppermute | solution.py:29
  125.1 7.3 %collective-permute-start.24 = (bf16[256,256]{1,0:T(8,128)(2,1)S(1)}, bf16[256,256]{1,0:T(8,128)(2,1)S(1)}, u32[]{:S(2)}, u32[]{:S(2)}) collective-permute-start(bf16[256,256]{1,0:T(8,128)(2,1)S(1)} %shard_map.144), channel_id=1, source_target_pairs={{0,32},{1,33},{2,34},{3,35},{4,36},{5,37},{6,38},{7,39},{8,40},{9,... | collective-permute-start | bytes 393224 | tf_op jit(solution)/shard_map/ppermute | solution.py:29
  127.2 8.2 %collective-permute-start.29 = (bf16[256,256]{1,0:T(8,128)(2,1)S(1)}, bf16[256,256]{1,0:T(8,128)(2,1)S(1)}, u32[]{:S(2)}, u32[]{:S(2)}) collective-permute-start(bf16[256,256]{1,0:T(8,128)(2,1)S(1)} %slice_bitcast_fusion), channel_id=1, source_target_pairs={{0,16},{1,17},{2,18},{3,19},{4,20},{5,21},{6,22},{7,23},{8,24},{9,... | collective-permute-start | bytes 393224 | tf_op jit(solution)/shard_map/ppermute | solution.py:29
  132.5 7.8 %collective-permute-start.28 = (bf16[256,256]{1,0:T(8,128)(2,1)S(1)}, bf16[256,256]{1,0:T(8,128)(2,1)S(1)}, u32[]{:S(2)}, u32[]{:S(2)}) collective-permute-start(bf16[256,256]{1,0:T(8,128)(2,1)S(1)} %shard_map.149), channel_id=1, source_target_pairs={{0,224},{1,225},{2,226},{3,227},{4,228},{5,229},{6,230},{7,231},{8... | collective-permute-start | bytes 393224 | tf_op jit(solution)/shard_map/ppermute | solution.py:29
  132.6 7.7 %collective-permute-start.27 = (bf16[256,256]{1,0:T(8,128)(2,1)S(1)}, bf16[256,256]{1,0:T(8,128)(2,1)S(1)}, u32[]{:S(2)}, u32[]{:S(2)}) collective-permute-start(bf16[256,256]{1,0:T(8,128)(2,1)S(1)} %shard_map.148), channel_id=1, source_target_pairs={{0,32},{1,33},{2,34},{3,35},{4,36},{5,37},{6,38},{7,39},{8,40},{9,... | collective-permute-start | bytes 393224 | tf_op jit(solution)/shard_map/ppermute | solution.py:29
  (19 other events, 192.2 us)

commit v3 on v2

--- a/solution.py
+++ b/solution.py
@@ -396,32 +396,24 @@
     )(own, t, up, down, y)
 
 
-def weights_kernel(pairs):
-    f = pairs[0].shape[1]
-
-    def body(*refs):
-        gs_ref, gn_ref, gb_ref = refs[-3:]
-        z, yl, yh, x, core = axes()
-        for j in range(NX):
-            at = (x + j) & (NX - 1)
-            rows = pl.ds(pl.multiple_of(at * 64, 64), 64)
-            for h, out in enumerate((gs_ref, gn_ref)):
-                start = pl.multiple_of((yh ^ h) * PART, 16)
-                out[rows, :] = refs[j][pl.ds(start, 64), :].astype(F32)
-
-            @pl.when(at == 0)
-            def _():
-                start = pl.multiple_of(yh * PART + 64, 16)
-                gb_ref[...] = refs[j][pl.ds(start, 16), :].astype(F32)[0:1]
+def weights_kernel(parts):
+    n, rows, f = parts.shape
+
+    def body(ref, gs_ref, gn_ref, gb_ref):
+        for d in range(n):
+            out = gs_ref if d < n // 2 else gn_ref
+            at = d % (n // 2) * 64
+            out[at : at + 64, :] = ref[d, 0:64, :].astype(F32)
+        gb_ref[...] = ref[0, 64:PART, :].astype(F32)[0:1]
 
     sq = jax.ShapeDtypeStruct((f, f), F32)
     return pl.pallas_call(
         body,
         out_shape=[sq, sq, jax.ShapeDtypeStruct((1, f), F32)],
-        in_specs=[VMEM] * NX,
+        in_specs=[VMEM],
         out_specs=[VMEM] * 3,
         compiler_params=params(16),
-    )(*pairs)
+    )(parts)
 
 
 def add(*terms):
@@ -503,19 +495,14 @@
         )
     )
     w = add(w, y1[2 * width :])
-    up4, down3, y0, w_y = together(
-        (
-            permute(hop_kernel([t1, y1], up3, False), dz=1),
-            permute(hop_kernel([t1d, (y1, slice(width, 2 * width))], down2, False), dz=-1),
-            permute(u1[:width], dyl=1),
-            permute(w, dyh=1),
-        )
-    )
+    up4 = permute(hop_kernel([t1, y1], up3, False), dz=1)
+    down3 = permute(hop_kernel([t1d, (y1, slice(width, 2 * width))], down2, False), dz=-1)
+    y0 = permute(u1[:width], dyl=1)
+    parts = jnp.broadcast_to(w[None], (len(chips[0]),) + w.shape)
+    parts = lax.all_to_all(parts, "rep", 0, 0, axis_index_groups=chips, tiled=True)
+    up4, down3, y0, parts = together((up4, down3, y0, parts))
     grad_features = features_kernel(own, t0, up4, down3, y0)
-    pair = join_kernel([w, w_y])
-    grad_self, grad_neigh, grad_bias = weights_kernel(
-        [pair, permute(pair, dx=-1), permute(pair, dx=2), permute(pair, dx=1)]
-    )
+    grad_self, grad_neigh, grad_bias = weights_kernel(parts)
     return (output, grad_features, grad_self, grad_neigh, grad_bias.reshape(width))
 
 

time: 150 us -> 147 us (0.980)
  waiting for transfers between devices: 35.1 us -> 31.6 us
  Pallas kernels: 16.7 us -> 18.8 us
  starting transfers between devices: 47.8 us -> 45.7 us
    ppermute x34 -> x30, waiting for transfers between devices: 35.1 us -> 29.4 us  [permute(): return lax.ppermute(value, ('blk', 'rep'), pairs)]
    ppermute x34 -> x30, starting transfers between devices: 47.8 us -> 42.2 us  [permute(): return lax.ppermute(value, ('blk', 'rep'), pairs)]
    all_to_all x0 -> x1, starting transfers between devices: none -> 3.5 us  [local(): lax.all_to_all(parts, 'rep', 0, 0, axis_index_groups=chips, tiled=True)]
    all_to_all x0 -> x1, waiting for transfers between devices: none -> 2.22 us  [local(): lax.all_to_all(parts, 'rep', 0, 0, axis_index_groups=chips, tiled=True)]
  transfers between devices with their start and end apart: 34 -> 31, of which waited for: 14 -> 15; matrix products, arithmetic and copies ran while one was open for 0% -> 0% of each run, Pallas kernels for 9% -> 10%
where the time goes in v3:
time: 147 us
  starting transfers between devices  45.7 us (31%)
  blocking collectives  45.7 us (31%)
  waiting for transfers between devices  31.6 us (21%)
  Pallas kernels  18.8 us (13%)
  local copies, waits for them, and re-layouts  3.75 us (3%)
    ppermute x30, starting transfers between devices, permute(): return lax.ppermute(value, ('blk', 'rep'), pairs)  42.2 us
    ppermute x30, waiting for transfers between devices, permute(): return lax.ppermute(value, ('blk', 'rep'), pairs)  29.4 us
    all_to_all x1, blocking collectives, local(): lax.all_to_all(half, 'rep', 0, 0, axis_index_groups=chips, tiled=True)  23.2 us
    all_to_all x1, blocking collectives, local(): lax.all_to_all(send, 'rep', 0, 0, axis_index_groups=chips, tiled=True)  22.6 us
    pallas_call x4, Pallas kernels, forward_kernel(): pl.pallas_call(body, out_shape=out_shape, in_specs=[SMEM] * 2 + [VMEM] *...  6.66 us
    pallas_call x4, Pallas kernels, backward_kernel(): pl.pallas_call(body, out_shape=[jax.ShapeDtypeStruct((width, 2 * TILE), B...  6.15 us
    all_to_all x1, starting transfers between devices, local(): lax.all_to_all(parts, 'rep', 0, 0, axis_index_groups=chips, tiled=True)  3.5 us
  transfers between devices with their start and end apart: 31, of which 15 were waited for; matrix products, arithmetic and copies ran while one was open for 0% of the time, Pallas kernels for 10%

profile of v3, /device:TPU:8, one launch (start us, length us, event | category | flops | bytes accessed | tf_op | source)
XLA Modules:
  0.0 146.9 jit_solution(862519972860401057)
XLA Ops:
  0.6 2.3 %collective-permute-start.4 = (bf16[256,256]{1,0:T(8,128)(2,1)}, bf16[256,256]{1,0:T(8,128)(2,1)S(1)}, u32[]{:S(2)}, u32[]{:S(2)}) collective-permute-start(bf16[256,256]{1,0:T(8,128)(2,1)} %x_ref.1), channel_id=1, source_target_pairs={{0,16},{1,17},{2,18},{3,19},{4,20},{5,21},{6,22},{7,23},{8,24},{9,... | collective-permute-start | bytes 393224 | tf_op jit(solution)/shard_map/ppermute | solution.py:29
  3.1 2.8 %copy-done = bf16[1,1,16,12,128,128]{5,4,3,2,1,0:T(8,128)(2,1)S(1)} copy-done((bf16[1,1,16,12,128,128]{5,4,3,2,1,0:T(8,128)(2,1)S(1)}, bf16[1,1,16,12,128,128]{5,4,3,2,1,0:T(8,128)(2,1)}, u32[]{:S(2)}) %copy-start) | copy-done | bytes 6291480
  6.3 5.7 %collective-permute-start.5 = (bf16[256,256]{1,0:T(8,128)(2,1)S(1)}, bf16[256,256]{1,0:T(8,128)(2,1)S(1)}, u32[]{:S(2)}, u32[]{:S(2)}) collective-permute-start(bf16[256,256]{1,0:T(8,128)(2,1)S(1)} %collective-permute-done.4.refs_1_), channel_id=1, source_target_pairs={{0,224},{1,225},{2,226},{3,227},{4,228},{5,229},{6,230},{7,231},{8... | collective-permute-start | bytes 393224 | tf_op jit(solution)/shard_map/ppermute | solution.py:29
  15.3 3.7 %collective-permute-start.6 = (bf16[256,256]{1,0:T(8,128)(2,1)S(1)}, bf16[256,256]{1,0:T(8,128)(2,1)S(1)}, u32[]{:S(2)}, u32[]{:S(2)}) collective-permute-start(bf16[256,256]{1,0:T(8,128)(2,1)S(1)} %collective-permute-done.5.refs_3_), channel_id=1, source_target_pairs={{0,224},{1,225},{2,226},{3,227},{4,228},{5,229},{6,230},{7,231},{8... | collective-permute-start | bytes 393224 | tf_op jit(solution)/shard_map/ppermute | solution.py:29
  19.0 2.4 %shard_map.128 = (s32[4,88]{1,0:T(4,128)S(1)}, s32[4]{0:T(128)S(1)}) custom-call(s32[12,16]{1,0:T(8,128)S(1)} %get-tuple-element.102.rows_ref, s32[12,16]{1,0:T(8,128)S(1)} %get-tuple-element.101.cols_ref, s32[16]{0:T(128)S(1)} %bitcast.23), custom_call_target="tpu_custom_call" | custom-call | tf_op jit(solution)/shard_map/pallas_call | solution.py:76
  25.4 3.7 %collective-permute-start.9 = (bf16[256,256]{1,0:T(8,128)(2,1)S(1)}, bf16[256,256]{1,0:T(8,128)(2,1)S(1)}, u32[]{:S(2)}, u32[]{:S(2)}) collective-permute-start(bf16[256,256]{1,0:T(8,128)(2,1)S(1)} %collective-permute-done.6.refs_1_), channel_id=1, source_target_pairs={{0,224},{1,225},{2,226},{3,227},{4,228},{5,229},{6,230},{7,231},{8... | collective-permute-start | bytes 393224 | tf_op jit(solution)/shard_map/ppermute | solution.py:29
  29.3 1.9 %collective-permute-start.14 = (bf16[256,256]{1,0:T(8,128)(2,1)S(1)}, bf16[256,256]{1,0:T(8,128)(2,1)S(1)}, u32[]{:S(2)}, u32[]{:S(2)}) collective-permute-start(bf16[256,256]{1,0:T(8,128)(2,1)S(1)} %collective-permute-done.11.refs_3_), channel_id=1, source_target_pairs={{0,32},{1,33},{2,34},{3,35},{4,36},{5,37},{6,38},{7,39},{8,40},{9,... | collective-permute-start | bytes 393224 | tf_op jit(solution)/shard_map/ppermute | solution.py:29
  31.2 2.0 %shard_map.131.refs_4_ = f32[33,128,256]{2,1,0:T(8,128)S(1)} custom-call(s32[4,88]{1,0:T(4,128)S(1)} %get-tuple-element.52.list_ref, s32[4]{0:T(128)S(1)} %get-tuple-element.53.len_ref, bf16[192,128,128]{2,1,0:T(8,128)(2,1)S(1)} %shard_map.129.a_ref, bf16[256,256]{1,0:T(8,128)(2,1)S(1)} %collective-permute-done.10.refs_0_, ...), custom_call_target="tpu_custom_call" | custom-call | flops 402653184 | bytes 655360 | tf_op jit(solution)/shard_map/pallas_call | solution.py:162
  33.2 3.2 %collective-permute-start.12 = (bf16[256,256]{1,0:T(8,128)(2,1)S(1)}, bf16[256,256]{1,0:T(8,128)(2,1)S(1)}, u32[]{:S(2)}, u32[]{:S(2)}) collective-permute-start(bf16[256,256]{1,0:T(8,128)(2,1)S(1)} %collective-permute-done.9.refs_1_), channel_id=1, source_target_pairs={{0,224},{1,225},{2,226},{3,227},{4,228},{5,229},{6,230},{7,231},{8... | collective-permute-start | bytes 393224 | tf_op jit(solution)/shard_map/ppermute | solution.py:29
  40.8 2.6 %collective-permute-done.15 = bf16[2048,256]{1,0:T(8,128)(2,1)S(1)} collective-permute-done((bf16[2048,256]{1,0:T(8,128)(2,1)S(1)}, bf16[2048,256]{1,0:T(8,128)(2,1)S(1)}, u32[]{:S(2)}, u32[]{:S(2)}) %collective-permute-start.15) | collective-permute-done | bytes 1048608 | tf_op jit(solution)/shard_map/ppermute | solution.py:29
  43.8 23.2 %all_to_all.15.parts_ref = bf16[8,256,256]{2,1,0:T(8,128)(2,1)S(1)} all-to-all(bf16[8,256,256]{2,1,0:T(8,128)(2,1)S(1)} %bitcast.24), channel_id=1, replica_groups={{0,2,4,6,8,10,12,14},{1,3,5,7,9,11,13,15},{16,18,20,22,24,26,28,30},{17..., dimensions={0} | all-to-all | bytes 2097152 | tf_op jit(solution)/shard_map/all_to_all | solution.py:458
  68.1 22.6 %all_to_all.16.ref = bf16[8,672,128]{2,1,0:T(8,128)(2,1)S(1)} all-to-all(bf16[8,672,128]{2,1,0:T(8,128)(2,1)S(1)} %get-tuple-element.62), channel_id=1, replica_groups={{0,2,4,6,8,10,12,14},{1,3,5,7,9,11,13,15},{16,18,20,22,24,26,28,30},{17..., dimensions={0} | all-to-all | bytes 2752512 | tf_op jit(solution)/shard_map/all_to_all | solution.py:462
  90.9 2.7 %collective-permute-done.16.their_ref.b_ref = bf16[4256,128]{1,0:T(8,128)(2,1)S(1)} collective-permute-done((bf16[4256,128]{1,0:T(8,128)(2,1)S(1)}, bf16[4256,128]{1,0:T(8,128)(2,1)S(1)}, u32[]{:S(2)}, u32[]{:S(2)}) %collective-permute-start.16) | collective-permute-done | bytes 1089568 | tf_op jit(solution)/shard_map/ppermute | solution.py:29
  93.6 4.7 %collective-permute-start.18 = (bf16[80,256]{1,0:T(8,128)(2,1)S(1)}, bf16[80,256]{1,0:T(8,128)(2,1)S(1)}, u32[]{:S(2)}, u32[]{:S(2)}) collective-permute-start(bf16[80,256]{1,0:T(8,128)(2,1)S(1)} %shard_map.137), channel_id=1, source_target_pairs={{0,128},{1,129},{2,130},{3,131},{4,132},{5,133},{6,134},{7,135},{8... | collective-permute-start | bytes 122888 | tf_op jit(solution)/shard_map/ppermute | solution.py:29
  101.7 3.2 %collective-permute-done.17.refs_1_ = bf16[1,256,256]{2,1,0:T(8,128)(2,1)S(1)} collective-permute-done((bf16[1,256,256]{2,1,0:T(8,128)(2,1)S(1)}, bf16[1,256,256]{2,1,0:T(8,128)(2,1)S(1)}, u32[]{:S(2)}, u32[]{:S(2)}) %collective-permute-start.17) | collective-permute-done | bytes 131104 | tf_op jit(solution)/shard_map/ppermute | solution.py:29
  107.5 5.3 %collective-permute-done.19.refs_2_.refs_1_ = bf16[336,256]{1,0:T(8,128)(2,1)S(1)} collective-permute-done((bf16[336,256]{1,0:T(8,128)(2,1)S(1)}, bf16[336,256]{1,0:T(8,128)(2,1)S(1)}, u32[]{:S(2)}, u32[]{:S(2)}) %collective-permute-start.19) | collective-permute-done | bytes 172064 | tf_op jit(solution)/shard_map/ppermute | solution.py:29
  114.5 2.1 %collective-permute-start.22 = (bf16[336,256]{1,0:T(8,128)(2,1)S(1)}, bf16[336,256]{1,0:T(8,128)(2,1)S(1)}, u32[]{:S(2)}, u32[]{:S(2)}) collective-permute-start(bf16[336,256]{1,0:T(8,128)(2,1)S(1)} %shard_map.143), channel_id=1, source_target_pairs={{0,224},{1,225},{2,226},{3,227},{4,228},{5,229},{6,230},{7,231},{8... | collective-permute-start | bytes 516104 | tf_op jit(solution)/shard_map/ppermute | solution.py:29
  120.0 3.6 %collective-permute-done.21.refs_2_ = bf16[336,256]{1,0:T(8,128)(2,1)S(1)} collective-permute-done((bf16[336,256]{1,0:T(8,128)(2,1)S(1)}, bf16[336,256]{1,0:T(8,128)(2,1)S(1)}, u32[]{:S(2)}, u32[]{:S(2)}) %collective-permute-start.21) | collective-permute-done | bytes 172064 | tf_op jit(solution)/shard_map/ppermute | solution.py:29
  125.7 2.1 %collective-permute-start.24 = (bf16[256,256]{1,0:T(8,128)(2,1)S(1)}, bf16[256,256]{1,0:T(8,128)(2,1)S(1)}, u32[]{:S(2)}, u32[]{:S(2)}) collective-permute-start(bf16[256,256]{1,0:T(8,128)(2,1)S(1)} %shard_map.144), channel_id=1, source_target_pairs={{0,32},{1,33},{2,34},{3,35},{4,36},{5,37},{6,38},{7,39},{8,40},{9,... | collective-permute-start | bytes 393224 | tf_op jit(solution)/shard_map/ppermute | solution.py:29
  127.8 2.8 %collective-permute-done.25.refs_2_ = bf16[256,256]{1,0:T(8,128)(2,1)S(1)} collective-permute-done((bf16[256,256]{1,0:T(8,128)(2,1)S(1)}, bf16[256,256]{1,0:T(8,128)(2,1)S(1)}, u32[]{:S(2)}, u32[]{:S(2)}) %collective-permute-start.25) | collective-permute-done | bytes 131104 | tf_op jit(solution)/shard_map/ppermute | solution.py:29
  132.7 3.5 %all-to-all-start.2 = ((bf16[8,80,256]{2,1,0:T(8,128)(2,1)}), bf16[8,80,256]{2,1,0:T(8,128)(2,1)S(1)}, u32[]{:S(2)}, u32[]{:S(2)}) async-start(bf16[8,80,256]{2,1,0:T(8,128)(2,1)} %broadcast_in_dim.2), calls=%async_computation.2 | async-start | bytes 655360 | tf_op jit(solution)/shard_map/all_to_all | solution.py:502
  136.9 2.1 %collective-permute-start.27 = (bf16[256,256]{1,0:T(8,128)(2,1)S(1)}, bf16[256,256]{1,0:T(8,128)(2,1)S(1)}, u32[]{:S(2)}, u32[]{:S(2)}) collective-permute-start(bf16[256,256]{1,0:T(8,128)(2,1)S(1)} %shard_map.148), channel_id=1, source_target_pairs={{0,32},{1,33},{2,34},{3,35},{4,36},{5,37},{6,38},{7,39},{8,40},{9,... | collective-permute-start | bytes 393224 | tf_op jit(solution)/shard_map/ppermute | solution.py:29
  138.9 2.8 %collective-permute-done.29.y_ref = bf16[256,256]{1,0:T(8,128)(2,1)S(1)} collective-permute-done((bf16[256,256]{1,0:T(8,128)(2,1)S(1)}, bf16[256,256]{1,0:T(8,128)(2,1)S(1)}, u32[]{:S(2)}, u32[]{:S(2)}) %collective-permute-start.29) | collective-permute-done | bytes 131104 | tf_op jit(solution)/shard_map/ppermute | solution.py:29
  143.1 2.2 %all-to-all-done.2.ref = bf16[8,80,256]{2,1,0:T(8,128)(2,1)S(1)} async-done(((bf16[8,80,256]{2,1,0:T(8,128)(2,1)}), bf16[8,80,256]{2,1,0:T(8,128)(2,1)S(1)}, u32[]{:S(2)}, u32[]{:S(2)}) %all-to-all-start.2) | async-done | bytes 327712 | tf_op jit(solution)/shard_map/all_to_all | solution.py:502
  (90 shorter events, 33.1 us)
Async XLA Ops:
  0.6 5.7 %collective-permute-start.4 = (bf16[256,256]{1,0:T(8,128)(2,1)}, bf16[256,256]{1,0:T(8,128)(2,1)S(1)}, u32[]{:S(2)}, u32[]{:S(2)}) collective-permute-start(bf16[256,256]{1,0:T(8,128)(2,1)} %x_ref.1), channel_id=1, source_target_pairs={{0,16},{1,17},{2,18},{3,19},{4,20},{5,21},{6,22},{7,23},{8,24},{9,... | collective-permute-start | bytes 393224 | tf_op jit(solution)/shard_map/ppermute | solution.py:29
  2.9 11.2 %collective-permute-start = (bf16[256,256]{1,0:T(8,128)(2,1)}, bf16[256,256]{1,0:T(8,128)(2,1)S(1)}, u32[]{:S(2)}, u32[]{:S(2)}) collective-permute-start(bf16[256,256]{1,0:T(8,128)(2,1)} %x_ref.1), channel_id=1, source_target_pairs={{0,32},{1,33},{2,34},{3,35},{4,36},{5,37},{6,38},{7,39},{8,40},{9,... | collective-permute-start | bytes 393224 | tf_op jit(solution)/shard_map/ppermute | solution.py:29
  6.3 9.0 %collective-permute-start.5 = (bf16[256,256]{1,0:T(8,128)(2,1)S(1)}, bf16[256,256]{1,0:T(8,128)(2,1)S(1)}, u32[]{:S(2)}, u32[]{:S(2)}) collective-permute-start(bf16[256,256]{1,0:T(8,128)(2,1)S(1)} %collective-permute-done.4.refs_1_), channel_id=1, source_target_pairs={{0,224},{1,225},{2,226},{3,227},{4,228},{5,229},{6,230},{7,231},{8... | collective-permute-start | bytes 393224 | tf_op jit(solution)/shard_map/ppermute | solution.py:29
  12.0 9.4 %collective-permute-start.7 = (bf16[256,256]{1,0:T(8,128)(2,1)S(1)}, bf16[256,256]{1,0:T(8,128)(2,1)S(1)}, u32[]{:S(2)}, u32[]{:S(2)}) collective-permute-start(bf16[256,256]{1,0:T(8,128)(2,1)S(1)} %copy-done.1), channel_id=1, source_target_pairs={{0,224},{1,225},{2,226},{3,227},{4,228},{5,229},{6,230},{7,231},{8... | collective-permute-start | bytes 393224 | tf_op jit(solution)/shard_map/ppermute | solution.py:29
  13.0 9.0 %collective-permute-start.8 = (bf16[256,256]{1,0:T(8,128)(2,1)S(1)}, bf16[256,256]{1,0:T(8,128)(2,1)S(1)}, u32[]{:S(2)}, u32[]{:S(2)}) collective-permute-start(bf16[256,256]{1,0:T(8,128)(2,1)S(1)} %collective-permute-done.4.refs_1_), channel_id=1, source_target_pairs={{0,32},{1,33},{2,34},{3,35},{4,36},{5,37},{6,38},{7,39},{8,40},{9,... | collective-permute-start | bytes 393224 | tf_op jit(solution)/shard_map/ppermute | solution.py:29
  14.1 9.4 %collective-permute-start.1 = (bf16[256,256]{1,0:T(8,128)(2,1)S(1)}, bf16[256,256]{1,0:T(8,128)(2,1)S(1)}, u32[]{:S(2)}, u32[]{:S(2)}) collective-permute-start(bf16[256,256]{1,0:T(8,128)(2,1)S(1)} %collective-permute-done.refs_4_), channel_id=1, source_target_pairs={{0,32},{1,33},{2,34},{3,35},{4,36},{5,37},{6,38},{7,39},{8,40},{9,... | collective-permute-start | bytes 393224 | tf_op jit(solution)/shard_map/ppermute | solution.py:29
  15.3 10.1 %collective-permute-start.6 = (bf16[256,256]{1,0:T(8,128)(2,1)S(1)}, bf16[256,256]{1,0:T(8,128)(2,1)S(1)}, u32[]{:S(2)}, u32[]{:S(2)}) collective-permute-start(bf16[256,256]{1,0:T(8,128)(2,1)S(1)} %collective-permute-done.5.refs_3_), channel_id=1, source_target_pairs={{0,224},{1,225},{2,226},{3,227},{4,228},{5,229},{6,230},{7,231},{8... | collective-permute-start | bytes 393224 | tf_op jit(solution)/shard_map/ppermute | solution.py:29
  21.4 7.7 %collective-permute-start.10 = (bf16[256,256]{1,0:T(8,128)(2,1)S(1)}, bf16[256,256]{1,0:T(8,128)(2,1)S(1)}, u32[]{:S(2)}, u32[]{:S(2)}) collective-permute-start(bf16[256,256]{1,0:T(8,128)(2,1)S(1)} %collective-permute-done.7.refs_2_), channel_id=1, source_target_pairs={{0,224},{1,225},{2,226},{3,227},{4,228},{5,229},{6,230},{7,231},{8... | collective-permute-start | bytes 393224 | tf_op jit(solution)/shard_map/ppermute | solution.py:29
  22.1 7.2 %collective-permute-start.11 = (bf16[256,256]{1,0:T(8,128)(2,1)S(1)}, bf16[256,256]{1,0:T(8,128)(2,1)S(1)}, u32[]{:S(2)}, u32[]{:S(2)}) collective-permute-start(bf16[256,256]{1,0:T(8,128)(2,1)S(1)} %collective-permute-done.8.refs_5_), channel_id=1, source_target_pairs={{0,32},{1,33},{2,34},{3,35},{4,36},{5,37},{6,38},{7,39},{8,40},{9,... | collective-permute-start | bytes 393224 | tf_op jit(solution)/shard_map/ppermute | solution.py:29
  23.5 7.6 %collective-permute-start.2 = (bf16[256,256]{1,0:T(8,128)(2,1)S(1)}, bf16[256,256]{1,0:T(8,128)(2,1)S(1)}, u32[]{:S(2)}, u32[]{:S(2)}) collective-permute-start(bf16[256,256]{1,0:T(8,128)(2,1)S(1)} %collective-permute-done.1.refs_2_), channel_id=1, source_target_pairs={{0,32},{1,33},{2,34},{3,35},{4,36},{5,37},{6,38},{7,39},{8,40},{9,... | collective-permute-start | bytes 393224 | tf_op jit(solution)/shard_map/ppermute | solution.py:29
  25.4 7.8 %collective-permute-start.9 = (bf16[256,256]{1,0:T(8,128)(2,1)S(1)}, bf16[256,256]{1,0:T(8,128)(2,1)S(1)}, u32[]{:S(2)}, u32[]{:S(2)}) collective-permute-start(bf16[256,256]{1,0:T(8,128)(2,1)S(1)} %collective-permute-done.6.refs_1_), channel_id=1, source_target_pairs={{0,224},{1,225},{2,226},{3,227},{4,228},{5,229},{6,230},{7,231},{8... | collective-permute-start | bytes 393224 | tf_op jit(solution)/shard_map/ppermute | solution.py:29
  29.1 7.3 %collective-permute-start.13 = (bf16[256,256]{1,0:T(8,128)(2,1)S(1)}, bf16[256,256]{1,0:T(8,128)(2,1)S(1)}, u32[]{:S(2)}, u32[]{:S(2)}) collective-permute-start(bf16[256,256]{1,0:T(8,128)(2,1)S(1)} %collective-permute-done.10.refs_0_), channel_id=1, source_target_pairs={{0,224},{1,225},{2,226},{3,227},{4,228},{5,229},{6,230},{7,231},{8... | collective-permute-start | bytes 393224 | tf_op jit(solution)/shard_map/ppermute | solution.py:29
  29.3 7.2 %collective-permute-start.14 = (bf16[256,256]{1,0:T(8,128)(2,1)S(1)}, bf16[256,256]{1,0:T(8,128)(2,1)S(1)}, u32[]{:S(2)}, u32[]{:S(2)}) collective-permute-start(bf16[256,256]{1,0:T(8,128)(2,1)S(1)} %collective-permute-done.11.refs_3_), channel_id=1, source_target_pairs={{0,32},{1,33},{2,34},{3,35},{4,36},{5,37},{6,38},{7,39},{8,40},{9,... | collective-permute-start | bytes 393224 | tf_op jit(solution)/shard_map/ppermute | solution.py:29
  31.1 6.7 %collective-permute-start.3 = (bf16[256,256]{1,0:T(8,128)(2,1)S(1)}, bf16[256,256]{1,0:T(8,128)(2,1)S(1)}, u32[]{:S(2)}, u32[]{:S(2)}) collective-permute-start(bf16[256,256]{1,0:T(8,128)(2,1)S(1)} %collective-permute-done.2.refs_2_), channel_id=1, source_target_pairs={{0,32},{1,33},{2,34},{3,35},{4,36},{5,37},{6,38},{7,39},{8,40},{9,... | collective-permute-start | bytes 393224 | tf_op jit(solution)/shard_map/ppermute | solution.py:29
  33.2 5.8 %collective-permute-start.12 = (bf16[256,256]{1,0:T(8,128)(2,1)S(1)}, bf16[256,256]{1,0:T(8,128)(2,1)S(1)}, u32[]{:S(2)}, u32[]{:S(2)}) collective-permute-start(bf16[256,256]{1,0:T(8,128)(2,1)S(1)} %collective-permute-done.9.refs_1_), channel_id=1, source_target_pairs={{0,224},{1,225},{2,226},{3,227},{4,228},{5,229},{6,230},{7,231},{8... | collective-permute-start | bytes 393224 | tf_op jit(solution)/shard_map/ppermute | solution.py:29
  93.6 8.1 %collective-permute-start.18 = (bf16[80,256]{1,0:T(8,128)(2,1)S(1)}, bf16[80,256]{1,0:T(8,128)(2,1)S(1)}, u32[]{:S(2)}, u32[]{:S(2)}) collective-permute-start(bf16[80,256]{1,0:T(8,128)(2,1)S(1)} %shard_map.137), channel_id=1, source_target_pairs={{0,128},{1,129},{2,130},{3,131},{4,132},{5,133},{6,134},{7,135},{8... | collective-permute-start | bytes 122888 | tf_op jit(solution)/shard_map/ppermute | solution.py:29
  104.9 7.9 %collective-permute-start.20 = (bf16[2,256,256]{2,1,0:T(8,128)(2,1)S(1)}, bf16[2,256,256]{2,1,0:T(8,128)(2,1)S(1)}, u32[]{:S(2)}, u32[]{:S(2)}) collective-permute-start(bf16[2,256,256]{2,1,0:T(8,128)(2,1)S(1)} %get-tuple-element.70), channel_id=1, source_target_pairs={{0,16},{1,17},{2,18},{3,19},{4,20},{5,21},{6,22},{7,23},{8,24},{9,... | collective-permute-start | bytes 786440 | tf_op jit(solution)/shard_map/ppermute | solution.py:29
  105.6 7.1 %collective-permute-start.19 = (bf16[336,256]{1,0:T(8,128)(2,1)S(1)}, bf16[336,256]{1,0:T(8,128)(2,1)S(1)}, u32[]{:S(2)}, u32[]{:S(2)}) collective-permute-start(bf16[336,256]{1,0:T(8,128)(2,1)S(1)} %shard_map.139), channel_id=1, source_target_pairs={{0,32},{1,33},{2,34},{3,35},{4,36},{5,37},{6,38},{7,39},{8,40},{9,... | collective-permute-start | bytes 516104 | tf_op jit(solution)/shard_map/ppermute | solution.py:29
  112.8 10.9 %collective-permute-start.23 = (bf16[2,256,256]{2,1,0:T(8,128)(2,1)S(1)}, bf16[2,256,256]{2,1,0:T(8,128)(2,1)S(1)}, u32[]{:S(2)}, u32[]{:S(2)}) collective-permute-start(bf16[2,256,256]{2,1,0:T(8,128)(2,1)S(1)} %get-tuple-element.81), channel_id=1, source_target_pairs={{0,16},{1,17},{2,18},{3,19},{4,20},{5,21},{6,22},{7,23},{8,24},{9,... | collective-permute-start | bytes 786440 | tf_op jit(solution)/shard_map/ppermute | solution.py:29
  116.7 6.9 %collective-permute-start.21 = (bf16[336,256]{1,0:T(8,128)(2,1)S(1)}, bf16[336,256]{1,0:T(8,128)(2,1)S(1)}, u32[]{:S(2)}, u32[]{:S(2)}) collective-permute-start(bf16[336,256]{1,0:T(8,128)(2,1)S(1)} %shard_map.142), channel_id=1, source_target_pairs={{0,32},{1,33},{2,34},{3,35},{4,36},{5,37},{6,38},{7,39},{8,40},{9,... | collective-permute-start | bytes 516104 | tf_op jit(solution)/shard_map/ppermute | solution.py:29
  123.7 8.2 %collective-permute-start.26 = (bf16[592,256]{1,0:T(8,128)(2,1)S(1)}, bf16[592,256]{1,0:T(8,128)(2,1)S(1)}, u32[]{:S(2)}, u32[]{:S(2)}) collective-permute-start(bf16[592,256]{1,0:T(8,128)(2,1)S(1)} %shard_map.147), channel_id=1, source_target_pairs={{0,16},{1,17},{2,18},{3,19},{4,20},{5,21},{6,22},{7,23},{8,24},{9,... | collective-permute-start | bytes 909320 | tf_op jit(solution)/shard_map/ppermute | solution.py:29
  125.7 6.3 %collective-permute-start.24 = (bf16[256,256]{1,0:T(8,128)(2,1)S(1)}, bf16[256,256]{1,0:T(8,128)(2,1)S(1)}, u32[]{:S(2)}, u32[]{:S(2)}) collective-permute-start(bf16[256,256]{1,0:T(8,128)(2,1)S(1)} %shard_map.144), channel_id=1, source_target_pairs={{0,32},{1,33},{2,34},{3,35},{4,36},{5,37},{6,38},{7,39},{8,40},{9,... | collective-permute-start | bytes 393224 | tf_op jit(solution)/shard_map/ppermute | solution.py:29
  132.7 12.6 %all-to-all-start.2 = ((bf16[8,80,256]{2,1,0:T(8,128)(2,1)}), bf16[8,80,256]{2,1,0:T(8,128)(2,1)S(1)}, u32[]{:S(2)}, u32[]{:S(2)}) async-start(bf16[8,80,256]{2,1,0:T(8,128)(2,1)} %broadcast_in_dim.2), calls=%async_computation.2 | async-start | bytes 655360 | tf_op jit(solution)/shard_map/all_to_all | solution.py:502
  136.9 6.3 %collective-permute-start.27 = (bf16[256,256]{1,0:T(8,128)(2,1)S(1)}, bf16[256,256]{1,0:T(8,128)(2,1)S(1)}, u32[]{:S(2)}, u32[]{:S(2)}) collective-permute-start(bf16[256,256]{1,0:T(8,128)(2,1)S(1)} %shard_map.148), channel_id=1, source_target_pairs={{0,32},{1,33},{2,34},{3,35},{4,36},{5,37},{6,38},{7,39},{8,40},{9,... | collective-permute-start | bytes 393224 | tf_op jit(solution)/shard_map/ppermute | solution.py:29
  (16 other events, 174.5 us)
